TPU v7x, 256 devices: a whole 4x4x8 slice. The times are simulated.
256 devices in a mesh: rep: 32 (over y_hi, z, core), fsdp: 8 (over x, y_lo).
Axes of the slice: x: 4, y: 4 (y_hi: 2, y_lo: 2; y = y_hi * 2 + y_lo), z: 8, core: 2. Of those that a mesh axis runs over, the one named last changes fastest.
Arguments:
- context: bfloat16 [65536, 2048], P(('rep', 'fsdp')), may hold values from -6 to 6
- cotangent: bfloat16 [65536, 4096], P(('rep', 'fsdp')), may hold values from -0.13183594 to 0.13183594
- out_weight: bfloat16 [2048, 4096], P('fsdp'), may hold values from -4 to 4
- error_buffer: bfloat16 [32, 2048, 4096], P('rep', 'fsdp'), may hold values from -1.5 to 1.5
- seed_basis: float32 [4096, 32], replicated, may hold values from -6 to 6
Outputs:
- ctx_grad: bfloat16 [65536, 2048], P(('rep', 'fsdp'))
- update: bfloat16 [2048, 4096], P('fsdp')
- new_error: bfloat16 [32, 2048, 4096], P('rep', 'fsdp')
- new_basis: float32 [4096, 32], replicated
All inputs are finite; a program needn't handle non-finite values.
Results may differ from a plain program's by a relative error of at most 0.019.
Values may be sent and summed in bfloat16 or wider, within the bound.
No kernel may reach another device: no remote copies, remote signals or barrier semaphores. Data moves between devices by JAX's collectives and lax.ppermute only.
A program may use at most 128 MiB of HBM per device.

v0:
```python
import jax
import jax.numpy as jnp
from jax import lax
from jax.sharding import PartitionSpec as P


def body(context, cotangent, out_weight, error_buffer, seed_basis):
    highest = lax.Precision.HIGHEST
    ctx_grad = jnp.einsum(
        "td,hd->th",
        cotangent,
        lax.all_gather(out_weight, "fsdp", axis=0, tiled=True),
        preferred_element_type=jnp.float32,
    ).astype(jnp.bfloat16)
    grad_rows = lax.psum_scatter(
        jnp.einsum("th,td->hd", context, cotangent, preferred_element_type=jnp.float32).astype(
            jnp.bfloat16
        ),
        "fsdp",
        scatter_dimension=0,
        tiled=True,
    ).astype(jnp.float32)
    merged = grad_rows + error_buffer[0].astype(jnp.float32)
    p_local = jnp.dot(merged, seed_basis, precision=highest)
    p_mean = lax.psum(p_local, "rep") / lax.axis_size("rep")
    gram_matrix = lax.psum(jnp.dot(p_mean.T, p_mean, precision=highest), "fsdp")
    cholesky_factor = jnp.linalg.cholesky(gram_matrix)
    p_basis = lax.linalg.triangular_solve(
        cholesky_factor, p_mean, left_side=False, lower=True, transpose_a=True
    )
    q_local = jnp.einsum("hd,hk->dk", merged, p_basis, precision=highest)
    new_basis = lax.psum(q_local, ("rep", "fsdp")) / lax.axis_size("rep")
    low_rank = jnp.dot(p_basis, new_basis.T, precision=highest)
    update = low_rank.astype(jnp.bfloat16)
    new_error = (merged - low_rank)[None].astype(jnp.bfloat16)
    return (ctx_grad, update, new_error, new_basis)


def solution(mesh):
    return jax.shard_map(
        body,
        mesh=mesh,
        in_specs=(
            P(("rep", "fsdp"), None),
            P(("rep", "fsdp"), None),
            P("fsdp", None),
            P("rep", "fsdp", None),
            P(),
        ),
        out_specs=(P(("rep", "fsdp"), None), P("fsdp", None), P("rep", "fsdp", None), P()),
        check_vma=False,
    )
```

profile of v0, /device:TPU:2, one launch (start us, length us, event | category | flops | bytes accessed | tf_op | source)
XLA Modules:
  0.0 956.1 jit_solution(13637791840540591853)
XLA Ops:
  7.2 0.0 copy-start
  7.2 0.0 reduce-scatter.2.cloned.1.call-start
  7.2 1.5 copy-done
  8.8 9.3 convolution_convert_fusion
  18.1 0.0 reduce-scatter.2.cloned.1.call-update
  18.1 0.0 copy-start.2
  18.1 0.0 all-gather.2.cloned.1.call-start
  18.1 0.7 all-gather.2.cloned.1.call-update
  18.9 0.0 all-reduce.2.cloned.1.call-start
  18.9 331.3 %reduce-scatter.2.cloned.1.call-done = bf16[256,4096]{1,0:T(8,128)(2,1)} async-done(((bf16[2048,4096]{1,0:T(8,128)(2,1)}), bf16[256,4096]{1,0:T(8,128)(2,1)}) %reduce-scatter.2.cloned.1.call-update) | async-done | bytes 2097168 | tf_op jit(solution)/shard_map/reduce_scatter | solution.py:15
  350.2 0.0 copy-done.2
  350.2 6.0 fusion.1
  356.2 136.7 %psum.21 = f32[256,32]{0,1:T(8,128)S(1)} all-reduce(f32[256,32]{0,1:T(8,128)S(1)} %fusion.1), channel_id=1, replica_groups=mesh['rep'=32,'fsdp'=8] {'rep'}, use_global_device_ids=true, to_apply=%region_1.0 | all-reduce | flops 8192 | bytes 65536 | tf_op jit(solution)/shard_map/psum | solution.py:25
  492.8 0.2 fusion.7
  493.0 40.1 %psum.22 = f32[32,32]{0,1:T(8,128)S(1)} all-reduce(f32[32,32]{0,1:T(8,128)S(1)} %fusion.7), channel_id=1, replica_groups=mesh['rep'=32,'fsdp'=8] {'fsdp'}, use_global_device_ids=true, to_apply=%region_2.0 | all-reduce | flops 1024 | bytes 8192 | tf_op jit(solution)/shard_map/psum | solution.py:26
  533.1 0.1 copy.10
  533.2 2.9 cholesky.16
  536.2 0.6 compare_reduce_fusion
  536.8 0.7 fusion.9
  537.5 2.4 custom-call.6
  539.9 0.2 fusion.5
  540.2 6.0 fusion
  546.2 0.0 all-reduce.2.cloned.1.call-update
  546.2 137.6 %all-gather.2.cloned.1.call-done = bf16[2048,4096]{1,0:T(8,128)(2,1)} async-done(((bf16[256,4096]{1,0:T(8,128)(2,1)}), bf16[2048,4096]{1,0:T(8,128)(2,1)}) %all-gather.2.cloned.1.call-update) | async-done | bytes 16777232 | tf_op jit(solution)/shard_map/all_gather | solution.py:12
  683.8 9.2 convolution_convert_fusion.1
  693.0 248.4 %all-reduce.2.cloned.1.call-done = f32[4096,32]{0,1:T(8,128)} async-done(((f32[4096,32]{0,1:T(8,128)}), f32[4096,32]{0,1:T(8,128)}) %all-reduce.2.cloned.1.call-update) | async-done | bytes 524304 | tf_op jit(solution)/shard_map/psum | solution.py:32
  941.5 1.1 broadcast_multiply_fusion
  942.5 0.0 copy-start.1
  942.5 7.0 fusion.2
  949.6 0.0 copy-done.1
  (2 shorter events, 0.0 us)
Async XLA Ops:
  7.2 1.6 copy-start
  7.2 343.0 %reduce-scatter.2.cloned.1.call-start = ((), (), s32[]{:S(2)}) async-start(), calls=%async_computation.2 | async-start | bytes 18874368 | tf_op jit(solution)/shard_map/reduce_scatter | solution.py:15
  18.1 332.1 %copy-start.2 = (f32[4096,32]{0,1:T(8,128)S(1)}, f32[4096,32]{0,1:T(8,128)}, u32[]{:S(2)}) copy-start(f32[4096,32]{0,1:T(8,128)} %param.9) | copy-start | bytes 1572868
  18.1 665.7 %all-gather.2.cloned.1.call-start = ((), (), s32[]{:S(2)}) async-start(), calls=%async_computation.1 | async-start | bytes 18874368 | tf_op jit(solution)/shard_map/all_gather | solution.py:12
  18.9 922.6 %all-reduce.2.cloned.1.call-start = ((), (), s32[]{:S(2)}) async-start(), calls=%async_computation.3 | async-start | bytes 1048576 | tf_op jit(solution)/shard_map/psum | solution.py:32
  942.5 7.0 copy-start.1
Sparse Core Ops, SparseCore 0:
  18.2 331.9 reduce-scatter.1
  352.0 331.8 all-gather.1
  689.8 251.5 all-reduce.1
where the time goes:
time: 956 us
  waiting for transfers between devices  718 us (75%)
  blocking collectives  177 us (19%)
  matrix products  37.9 us (4%)
  between operations  13.8 us (1%)
    reduce_scatter x1, waiting for transfers between devices, body(): lax.psum_scatter(jnp.einsum('th,td->hd', context, cotangent, preferred_el...  331 us
    psum x1, waiting for transfers between devices, body(): new_basis = lax.psum(q_local, ('rep', 'fsdp')) / lax.axis_size('rep')  248 us
    all_gather x1, waiting for transfers between devices, body(): lax.all_gather(out_weight, 'fsdp', axis=0, tiled=True)  138 us
    psum x1, blocking collectives, body(): p_mean = lax.psum(p_local, 'rep') / lax.axis_size('rep')  137 us
    psum x1, blocking collectives, body(): gram_matrix = lax.psum(jnp.dot(p_mean.T, p_mean, precision=highest), 'fsdp')  40.1 us
  transfers between devices with their start and end apart: 3, of which 3 were waited for; matrix products, arithmetic and copies ran while one was open for 3% of the time, Pallas kernels for 0%

commit v1 on v0

v1 whole, which is shorter than its diff:
```python
import functools

import jax
import jax.numpy as jnp
from jax import lax
from jax.experimental import pallas as pl
from jax.experimental.pallas import tpu as pltpu
from jax.sharding import Mesh
from jax.sharding import PartitionSpec as P

AXES = ("yh", "z", "c", "x", "yl")
FSDP = ("x", "yl")
REP = ("yh", "z", "c")
F32 = jnp.float32
BF16 = jnp.bfloat16
SWAP = [(0, 1), (1, 0)]
TOK = 256
ROWS = 256
HD = 2048
DIM = 4096
RANK = 32
N_REP = 32
SPLIT = (2560, 1536)
STARTS = (0, 2560)
TILE = 512
FTILE = 512
VMEM = 60 << 20
NT = (((1,), (1,)), ((), ()))
NN = (((1,), (0,)), ((), ()))
TN = (((0,), (0,)), ((), ()))
RIGHT = [(0, 1), (1, 2), (2, 3), (3, 0)]
LEFT = [(1, 0), (2, 1), (3, 2), (0, 3)]
OPPOSITE = [(0, 2), (1, 3), (2, 0), (3, 1)]
fence = lax.optimization_barrier


def dot(a, b, dims):
    return lax.dot_general(a, b, dims, preferred_element_type=F32)


def terms(a):
    hi = a.astype(BF16)
    rest = a - hi.astype(F32)
    mid = rest.astype(BF16)
    return hi, mid, (rest - mid.astype(F32)).astype(BF16)


def split3(a):
    return jnp.concatenate(terms(a), axis=0)


def fold3(a):
    n = a.shape[0] // 3
    return a[:n] + (a[n : 2 * n] + a[2 * n :])


def left6(a):
    hi, mid, low = terms(a)
    return jnp.concatenate([hi, hi, mid, hi, mid, low], axis=0)


def right6(a):
    hi, mid, low = terms(a)
    return jnp.concatenate([hi, mid, hi, low, mid, hi], axis=0)


def params(size=VMEM):
    return pltpu.CompilerParams(vmem_limit_bytes=size)


def cost(flops, size):
    return pl.CostEstimate(flops=flops, bytes_accessed=size, transcendentals=0)


def to_tiles(src, row, out):
    lanes = src.shape[1] // 128
    for i in range(2):
        part = src[pl.ds(pl.multiple_of(row + 8 * i, 8), 8), :]
        for j in range(lanes):
            out[i * lanes + j] = part[:, j * 128 : (j + 1) * 128]


def from_tiles(t, row, dst):
    lanes = dst.shape[1] // 128
    for i in range(2):
        for j in range(lanes):
            dst[pl.ds(pl.multiple_of(row + 8 * i, 8), 8), j * 128 : (j + 1) * 128] = t[
                i * lanes + j
            ]


def copies(sems, pairs):
    started = []
    for i, (src, dst) in enumerate(pairs):
        copy = pltpu.make_async_copy(src, dst, sems.at[i])
        copy.start()
        started.append(copy)
    return started


def wait(started):
    for copy in started:
        copy.wait()


def call(kernel, name, ins, outs, scratch, flops, size, alias=None):
    spec = lambda inside: pl.BlockSpec(memory_space=pltpu.VMEM if inside else pl.ANY)
    return pl.pallas_call(
        kernel,
        in_specs=[pl.BlockSpec(memory_space=pltpu.SMEM)] + [spec(i) for _, i in ins[1:]],
        out_specs=[spec(i) for _, _, i in outs],
        out_shape=[jax.ShapeDtypeStruct(shape, dtype) for shape, dtype, _ in outs],
        scratch_shapes=scratch,
        input_output_aliases=alias or {},
        compiler_params=params(),
        cost_estimate=cost(flops, size),
        name=name,
    )(*[a for a, _ in ins])


DMA = lambda n: pltpu.SemaphoreType.DMA((n,))
PART = 1024
PARTS = DIM // PART


def left_kernel(at, seed, cot, err, ctx, keep, send, seed_v, cot_v, err_v, ctx_v, p, sems):
    sides = [slice(j * PART, (j + 1) * PART) for j in range(PARTS)]
    started = copies(
        sems,
        [(a.at[:, s], b.at[:, s]) for s in sides for a, b in ((seed, seed_v), (cot, cot_v), (err, err_v))]
        + [(ctx, ctx_v)],
    )
    u = e = 0.0
    for j, s in enumerate(sides):
        wait(started[3 * j : 3 * j + 3])
        s3 = split3(seed_v[:, s])
        u += dot(s3, cot_v[:, s], NT)
        e += dot(s3, err_v[:, s], NT)
    wait(started[-1:])
    p[...] = fold3(dot(split3(fold3(u)), ctx_v[...], NN))
    cols = pl.ds(pl.multiple_of((at[0] * 2 + at[1]) * ROWS, ROWS), ROWS)
    p[:, cols] += fold3(e)
    to_tiles(p, at[2] * 16, keep)
    to_tiles(p, (1 - at[2]) * 16, send)


def left_part(at, seed_t, cot, err, ctx):
    out = ((HD // 64, 8, 128), F32, True)
    return call(
        left_kernel,
        "left_part",
        [(at, True), (seed_t, False), (cot, False), (err, False), (ctx, False)],
        [out, out],
        [
            pltpu.VMEM((RANK, DIM), F32),
            pltpu.VMEM((TOK, DIM), BF16),
            pltpu.VMEM((ROWS, DIM), BF16),
            pltpu.VMEM((TOK, HD), BF16),
            pltpu.VMEM((RANK, HD), F32),
            DMA(3 * PARTS + 1),
        ],
        2 * 256 * 256 * 4096 * 3,
        6 << 20,
    )


def right_kernel(
    at, own, other, ctx, cot, err, keep, send, gram, rows, ctx_v, cot_v, err_v, p, q, sems
):
    sides = [slice(j * PART, (j + 1) * PART) for j in range(PARTS)]
    started = copies(
        sems,
        [(ctx, ctx_v)]
        + [(a.at[:, s], b.at[:, s]) for s in sides for a, b in ((cot, cot_v), (err, err_v))],
    )
    from_tiles(own, at[2] * 16, p)
    from_tiles(other, (1 - at[2]) * 16, p)
    p[...] = p[...] * (1.0 / N_REP)
    p3 = split3(p[...])
    mine = p[:, pl.ds(pl.multiple_of((at[0] * 2 + at[1]) * ROWS, ROWS), ROWS)]
    rows[...] = mine
    r3 = split3(mine)
    full = dot(p3, p3, NT)
    full = full[:RANK] + (full[RANK : 2 * RANK] + full[2 * RANK :])
    gram[...] = full[:, :RANK] + (full[:, RANK : 2 * RANK] + full[:, 2 * RANK :])
    wait(started[:1])
    v3 = split3(fold3(dot(p3, ctx_v[...], NT)))
    for j, s in enumerate(sides):
        wait(started[1 + 2 * j : 3 + 2 * j])
        q[:, s] = fold3(dot(v3, cot_v[:, s], NN) + dot(r3, err_v[:, s], NN))
    to_tiles(q, at[2] * 16, keep)
    to_tiles(q, (1 - at[2]) * 16, send)


def right_part(at, own, other, ctx, cot, err):
    out = ((DIM // 64, 8, 128), F32, True)
    return call(
        right_kernel,
        "right_part",
        [(at, True), (own, True), (other, True), (ctx, False), (cot, False), (err, False)],
        [out, out, ((RANK, RANK), F32, True), ((RANK, ROWS), F32, True)],
        [
            pltpu.VMEM((TOK, HD), BF16),
            pltpu.VMEM((TOK, DIM), BF16),
            pltpu.VMEM((ROWS, DIM), BF16),
            pltpu.VMEM((RANK, HD), F32),
            pltpu.VMEM((RANK, DIM), F32),
            DMA(2 * PARTS + 1),
        ],
        2 * 256 * 256 * 4096 * 3,
        6 << 20,
    )


def quarters_kernel(at, ctx, *rest):
    outs, ctx_v, sems = rest[:4], rest[4], rest[5]
    wait(copies(sems, [(ctx, ctx_v)]))
    for out, k in zip(outs, (0, 1, 3, 2)):
        lane = pl.multiple_of(lax.rem(at[0] + k, 4) * 2 * ROWS, 2 * ROWS)
        out[...] = ctx_v[:, pl.ds(lane, 2 * ROWS)].T


def quarters(at, ctx):
    return call(
        quarters_kernel,
        "quarters",
        [(at, True), (ctx, False)],
        [((2 * ROWS, TOK), BF16, True)] * 4,
        [pltpu.VMEM((TOK, HD), BF16), DMA(1)],
        0,
        2 << 20,
    )


def pick_kernel(at, src, dst, sems):
    n, cols = dst.shape
    rows = pl.ds(pl.multiple_of(at[2] * n, n), n)
    width = cols // 4
    sides = [pl.ds(i * width, width) for i in range(4)]
    wait(copies(sems, [(src.at[rows, s], dst.at[:, s]) for s in sides]))


def pick_half(at, a):
    rows, cols = a.shape
    outs = [((rows // 2, cols), a.dtype, True)]
    return call(pick_kernel, "pick_half", [(at, True), (a, False)], outs, [DMA(4)], 0, 2 << 20)[0]


def place_kernel(at, *refs):
    parts, dst, sems = refs[:4], refs[4], refs[5]
    width = parts[0].shape[1]
    pairs = []
    for part, k in zip(parts, (0, 3, 1, 2)):
        lane = pl.multiple_of(lax.rem(at[0] + k, 4) * width, width)
        pairs.append((part, dst.at[:, pl.ds(lane, width)]))
    wait(copies(sems, pairs))


def place(at, parts):
    tok, width = parts[0].shape
    ins = [(at, True)] + [(a, False) for a in parts]
    outs = [((tok, 4 * width), BF16, True)]
    return call(place_kernel, "place", ins, outs, [DMA(4)], 0, 2 << 20)[0]


def block_pairs(at, start, j, cot, others, buf, tile=None):
    here = pl.ds(j * TILE, TILE)
    tile = j if tile is None else tile
    pairs = [(cot.at[:, pl.ds(start + j * TILE, TILE)], buf.at[tile, pl.ds(0, TOK)])]
    for i, k in enumerate((3, 1, 2)):
        src = others[0].at[lax.rem(at[0] + k, 4), :, here] if len(others) == 1 else others[i].at[:, here]
        pairs.append((src, buf.at[tile, pl.ds((i + 1) * TOK, TOK)]))
    return pairs


def grad_kernel(start, count, n, at, *refs):
    ctx, cot, err, others = refs[:4], refs[4], refs[5], refs[6 : 6 + n]
    kept, sent, lhs, buf, err_v, out_k, out_s, in_sems, out_sems = refs[-9:]
    yl = at[1]
    pairs = []
    for k, block in enumerate(ctx):
        for i, row in enumerate((yl, 1 - yl)):
            rows = pl.ds(pl.multiple_of(row * ROWS, ROWS), ROWS)
            to = lhs.at[pl.ds(i * ROWS, ROWS), pl.ds(k * TOK, TOK)]
            pairs.append((block.at[rows, :], to))
    for j in range(count):
        pairs += block_pairs(at, start, j, cot, others, buf)
        pairs.append((err.at[:, pl.ds(start + j * TILE, TILE)], err_v.at[j]))
    started = copies(in_sems, pairs)
    wait(started[:8])
    done = []
    for j in range(count):
        wait(started[8 + 5 * j : 13 + 5 * j])
        out = dot(lhs[...], buf[j], NN)
        out_k[j] = (out[:ROWS] + err_v[j].astype(F32)).astype(BF16)
        out_s[j] = out[ROWS:].astype(BF16)
        done += copies(
            out_sems.at[pl.ds(2 * j, 2)],
            [
                (out_k.at[j], kept.at[:, pl.ds(j * TILE, TILE)]),
                (out_s.at[j], sent.at[:, pl.ds(j * TILE, TILE)]),
            ],
        )
    wait(done)


def grad_chunk(at, ctx, cot, err, others, start):
    width = others[0].shape[-1]
    count = width // TILE
    return call(
        functools.partial(grad_kernel, start, count, len(others)),
        "grad_chunk",
        [(at, True)] + [(a, False) for a in (*ctx, cot, err, *others)],
        [((ROWS, width), BF16, False), ((ROWS, width), BF16, False)],
        [
            pltpu.VMEM((2 * ROWS, 4 * TOK), BF16),
            pltpu.VMEM((count, 4 * TOK, TILE), BF16),
            pltpu.VMEM((count, ROWS, TILE), BF16),
            pltpu.VMEM((count, ROWS, TILE), BF16),
            pltpu.VMEM((count, ROWS, TILE), BF16),
            DMA(8 + 5 * count),
            DMA(2 * count),
        ],
        2 * 512 * 1024 * width,
        4 * 1024 * width,
    )


def ctx_kernel(sizes, at, cot, w_own, w_half, w_other, *refs):
    outs, (buf, wbuf, acc, sems) = refs[-8:-4], refs[-4:]
    pairs = []
    tile = 0
    for n, start, width in sizes:
        others, refs = refs[:n], refs[n:]
        for j in range(width // TILE):
            pairs += block_pairs(at, start, j, cot, others, buf, tile)
            cols = pl.ds(start + j * TILE, TILE)
            half = ROWS // 2
            for w, row, m in ((w_own, 0, ROWS), (w_half, ROWS, half), (w_other, ROWS + half, half)):
                pairs.append((w.at[:, cols], wbuf.at[tile, pl.ds(row, m)]))
            tile += 1
    started = copies(sems, pairs)
    for j in range(tile):
        wait(started[7 * j : 7 * j + 7])
        part = dot(buf[j], wbuf[j], NT)
        if j == 0:
            acc[...] = part
        else:
            acc[...] += part
    yl, c = at[1], at[2]
    half = ROWS // 2
    mine = pl.ds(pl.multiple_of(yl * ROWS, ROWS), ROWS)
    for k, out in enumerate(outs):
        tok = slice(k * TOK, (k + 1) * TOK)
        out[:, mine] = acc[tok, :ROWS].astype(BF16)
        for i, h in enumerate((c, 1 - c)):
            lane = pl.multiple_of((1 - yl) * ROWS + h * half, half)
            out[:, pl.ds(lane, half)] = acc[tok, ROWS + i * half : ROWS + (i + 1) * half].astype(
                BF16
            )


def ctx_blocks(at, cot, groups, weights):
    sizes = [(len(others), start, others[0].shape[-1]) for start, others in groups]
    count = DIM // TILE
    flat = [a for _, others in groups for a in others]
    return call(
        functools.partial(ctx_kernel, sizes),
        "ctx_blocks",
        [(at, True)] + [(a, False) for a in (cot, *weights, *flat)],
        [((TOK, 2 * ROWS), BF16, True)] * 4,
        [
            pltpu.VMEM((count, 4 * TOK, TILE), BF16),
            pltpu.VMEM((count, 2 * ROWS, TILE), BF16),
            pltpu.VMEM((4 * TOK, 2 * ROWS), F32),
            DMA(7 * count),
        ],
        2 * 512 * 1024 * DIM,
        4 * 1024 * DIM,
    )


def final_kernel(at, inv, rows, own, other, *refs):
    n = len(SPLIT)
    kept, got = refs[:n], refs[n : 2 * n]
    basis, update, new_err, q, kept_v, got_v, up_v, new_v, in_sems, out_sems = refs[2 * n :]
    sides = [slice(j * FTILE, (j + 1) * FTILE) for j in range(DIM // FTILE)]
    pairs = []
    for j, s in enumerate(sides):
        i = max(i for i in range(n) if STARTS[i] <= s.start)
        src = pl.ds(s.start - STARTS[i], FTILE)
        pairs += [(kept[i].at[:, src], kept_v.at[j]), (got[i].at[:, src], got_v.at[j])]
    started = copies(in_sems, pairs)
    from_tiles(own, at[2] * 16, q)
    from_tiles(other, (1 - at[2]) * 16, q)
    inv6 = left6(inv[...].T)
    pb = left6(dot(inv6, right6(rows[...]), TN))
    done = []
    for j, s in enumerate(sides):
        nb = dot(inv6, right6(q[:, s]), TN) * (1.0 / N_REP)
        basis[:, s] = nb
        low = dot(pb, right6(nb), TN)
        up_v[j] = low.astype(BF16)
        wait(started[2 * j : 2 * j + 2])
        new_v[j] = (kept_v[j].astype(F32) + got_v[j].astype(F32) - low).astype(BF16)
        here = pl.ds(s.start, FTILE)
        done += copies(
            out_sems.at[pl.ds(2 * j, 2)],
            [(up_v.at[j], update.at[:, here]), (new_v.at[j], new_err.at[:, here])],
        )
    wait(done)


def final_part(at, inv, rows, own, other, kept, got):
    n = DIM // FTILE
    return call(
        final_kernel,
        "final_part",
        [(at, True), (inv, True), (rows, True), (own, True), (other, True)]
        + [(a, False) for a in (*kept, *got)],
        [((RANK, DIM), F32, True), ((ROWS, DIM), BF16, False), ((ROWS, DIM), BF16, False)],
        [pltpu.VMEM((RANK, DIM), F32)]
        + [pltpu.VMEM((n, ROWS, FTILE), BF16)] * 4
        + [DMA(2 * n), DMA(2 * n)],
        2 * 256 * 256 * 4096,
        8 << 20,
    )


def spread(t, axes):
    n = lax.axis_size(axes)
    return lax.all_to_all(t, axes, 0, 0, tiled=True).reshape(n, -1, 8, 128)


def collect(m, axes):
    n = lax.axis_size(axes)
    return spread(jnp.broadcast_to(m[None], (n,) + m.shape).reshape(-1, 8, 128), axes)


def body(context, cotangent, out_weight, error_buffer, seed_basis):
    x, yl, c = lax.axis_index("x"), lax.axis_index("yl"), lax.axis_index("c")
    at = jnp.stack([x, yl, c]).astype(jnp.int32)
    error = error_buffer[0]

    keep, send = left_part(at, seed_basis.T, cotangent, error, context)
    keep, send, cot, ctx, weight = fence((keep, send, cotangent, context, out_weight))

    wide_a, wide_b = [
        [lax.all_gather(cot[:, a : a + n], "x", axis=0)] for a, n in zip(STARTS, SPLIT)
    ]

    moved = quarters(at, ctx)
    perms = (RIGHT, LEFT, OPPOSITE)
    ctx_x = [moved[0]] + [lax.ppermute(m, "x", p) for m, p in zip(moved[1:], perms)]
    got = spread(keep + lax.ppermute(send, "c", SWAP), "z")
    half = pick_half(at, weight)
    got, ctx_x, half = fence((got, ctx_x, half))

    got = collect(jnp.sum(got, 0), ("yh", "x", "yl"))
    got, half = fence((got, half))

    pt = collect(jnp.sum(got, 0), "z").reshape(-1, 8, 128)
    pt, half = fence((pt, half))
    half = lax.ppermute(half, "yl", SWAP)
    po = lax.ppermute(pt, "c", SWAP)

    keep, send, gram, p_rows = right_part(at, pt, po, context, cotangent, error)
    keep, send, gram = fence((keep, send, gram))
    got = spread(keep + lax.ppermute(send, "c", SWAP), "z")
    kept_a, sent_a = grad_chunk(at, ctx_x, cotangent, error, wide_a, STARTS[0])
    got, kept_a, sent_a, half = fence((got, kept_a, sent_a, half))

    got_a = lax.ppermute(sent_a, "yl", SWAP)
    other = lax.ppermute(half, "c", SWAP)
    got = collect(jnp.sum(got, 0), ("yh", "x", "yl"))
    chol = jnp.linalg.cholesky(gram)
    inv = lax.linalg.triangular_solve(
        chol, jnp.eye(RANK, dtype=F32), left_side=True, lower=True
    )
    got, got_a, inv, other = fence((got, got_a, inv, other))

    qt = collect(jnp.sum(got, 0), "z").reshape(-1, 8, 128)
    kept_b, sent_b = grad_chunk(at, ctx_x, cotangent, error, wide_b, STARTS[1])
    qt, kept_b, sent_b = fence((qt, kept_b, sent_b))

    got_b = lax.ppermute(sent_b, "yl", SWAP)
    qo = lax.ppermute(qt, "c", SWAP)
    groups = list(zip(STARTS, (wide_a, wide_b)))
    blocks = ctx_blocks(at, cotangent, groups, [weight, half, other])
    got_b, qo, blocks = fence((got_b, qo, blocks))
    back = (LEFT, RIGHT, OPPOSITE)
    home = [blocks[0]] + [lax.ppermute(m, "x", p) for m, p in zip(blocks[1:], back)]
    new_basis, update, new_error = final_part(
        at, inv, p_rows, qt, qo, (kept_a, kept_b), (got_a, got_b)
    )
    ctx_grad = place(at, [home[0], home[2], home[1], home[3]])
    return (ctx_grad, update, new_error[None], new_basis.T)


def solution(mesh):
    fine = Mesh(mesh.devices.reshape(2, 8, 2, 4, 2), AXES)
    return jax.shard_map(
        body,
        mesh=fine,
        in_specs=(P(AXES, None), P(AXES, None), P(FSDP, None), P(REP, FSDP, None), P()),
        out_specs=(P(AXES, None), P(FSDP, None), P(REP, FSDP, None), P()),
        check_vma=False,
    )
```

time: 956 us -> 192 us (0.20)
  waiting for transfers between devices: 718 us -> 50 us
  blocking collectives: 177 us -> 29.1 us
  Pallas kernels: 0 us -> 47.6 us
  matrix products: 37.9 us -> 0.83 us
  starting transfers between devices: 0.12 us -> 33.1 us
    reduce_scatter x1 -> x0, waiting for transfers between devices: 331 us -> none  [body(): lax.psum_scatter(jnp.einsum('th,td->hd', context, cotangent, preferred_el...]
    psum x1 -> x0, waiting for transfers between devices: 248 us -> none  [body(): new_basis = lax.psum(q_local, ('rep', 'fsdp')) / lax.axis_size('rep')]
    psum x2 -> x0, blocking collectives: 177 us -> none  [the longest x1 137 us: body(): p_mean = lax.psum(p_local, 'rep') / lax.axis_size('rep')]
    all_gather x1 -> x2, waiting for transfers between devices: 138 us -> 0.04 us  [body(): lax.all_gather(cot[:, a:a + n], 'x', axis=0)]
    pallas_call x0 -> x9, Pallas kernels: none -> 47.6 us  [call(): pl.pallas_call(kernel, in_specs=[pl.BlockSpec(memory_space=pltpu.SMEM)] +...]
    dot_general x6 -> x0, matrix products: 37.7 us -> none  [the longest x1 9.3 us: body(): jnp.einsum('th,td->hd', context, cotangent, preferred_element_type=jnp.fl...]
    all_to_all x0 -> x4, waiting for transfers between devices: none -> 36.7 us  [spread(): return lax.all_to_all(t, axes, 0, 0, tiled=True).reshape(n, -1, 8, 128)]
    all_to_all x0 -> x2, blocking collectives: none -> 29.1 us  [spread(): return lax.all_to_all(t, axes, 0, 0, tiled=True).reshape(n, -1, 8, 128)]
  transfers between devices with their start and end apart: 3 -> 20, of which waited for: 3 -> 9; matrix products, arithmetic and copies ran while one was open for 3% -> 7% of each run, Pallas kernels for 0% -> 21%
where the time goes in v1:
time: 192 us; the launch traced here: 190 us
  waiting for transfers between devices  50 us (26%)
  Pallas kernels  47.6 us (25%)
  starting transfers between devices  33.1 us (17%)
  blocking collectives  29.1 us (15%)
  between operations  14.4 us (8%)
  other arithmetic  9.84 us (5%)
  local copies, waits for them, and re-layouts  5.26 us (3%)
    pallas_call x9, Pallas kernels, call(): pl.pallas_call(kernel, in_specs=[pl.BlockSpec(memory_space=pltpu.SMEM)] +...  47.6 us
    all_to_all x4, waiting for transfers between devices, spread(): return lax.all_to_all(t, axes, 0, 0, tiled=True).reshape(n, -1, 8, 128)  36.7 us
    all_to_all x2, blocking collectives, spread(): return lax.all_to_all(t, axes, 0, 0, tiled=True).reshape(n, -1, 8, 128)  29.1 us
    all_to_all x4, starting transfers between devices, spread(): return lax.all_to_all(t, axes, 0, 0, tiled=True).reshape(n, -1, 8, 128)  21.5 us
    ppermute x6, starting transfers between devices, body(): lax.ppermute(m, 'x', p)  8.65 us
    ppermute x1, waiting for transfers between devices, body(): got_b = lax.ppermute(sent_b, 'yl', SWAP)  7.51 us
  transfers between devices with their start and end apart: 20, of which 9 were waited for; matrix products, arithmetic and copies ran while one was open for 7% of the time, Pallas kernels for 21%

profile of v1, /device:TPU:2, one launch (start us, length us, event | category | flops | bytes accessed | tf_op | source)
XLA Modules:
  0.0 190.1 jit_solution(4560391553840428634)
XLA Ops:
  7.2 0.0 all-gather.5.cloned.1.call-start
  7.2 0.7 pad_add_fusion.at
  7.9 5.0 %left_part.1 = (f32[32,8,128]{2,1,0:T(8,128)}, f32[32,8,128]{2,1,0:T(8,128)}) custom-call(s32[3]{0:T(128)} %pad_add_fusion.at, f32[32,4096]{1,0:T(8,128)} %bitcast.41, bf16[256,4096]{1,0:T(8,128)(2,1)} %cot.5, bf16[256,4096]{1,0:T(8,128)(2,1)} %bitcast.26, bf16[256,2048]{1,0:T(8,128)(2,1)} %ctx.4), custom_call_target="tpu_custom_call" | custom-call | flops 1610612736 | bytes 6291456 | tf_op jit(solution)/shard_map/left_part/pallas_call | solution.py:108
  12.9 1.2 slice.16
  14.1 0.0 all-gather.5.cloned.1.call-update
  14.1 0.0 all-gather.7.cloned.1.call-start
  14.2 0.9 slice.17
  15.1 0.0 all-gather.7.cloned.1.call-update
  15.1 0.1 collective-permute-start
  15.2 3.0 %quarters.1 = (bf16[512,256]{1,0:T(8,128)(2,1)}, bf16[512,256]{1,0:T(8,128)(2,1)}, bf16[512,256]{1,0:T(8,128)(2,1)}, bf16[512,256]{1,0:T(8,128)(2,1)}) custom-call(s32[3]{0:T(128)} %pad_add_fusion.at, bf16[256,2048]{1,0:T(8,128)(2,1)} %ctx.4), custom_call_target="tpu_custom_call" | custom-call | bytes 2097152 | tf_op jit(solution)/shard_map/quarters/pallas_call | solution.py:108
  18.2 1.6 collective-permute-start.1
  19.8 0.9 collective-permute-start.2
  20.7 2.0 %collective-permute-start.3 = (bf16[512,256]{1,0:T(8,128)(2,1)}, bf16[512,256]{1,0:T(8,128)(2,1)S(1)}, u32[]{:S(2)}, u32[]{:S(2)}) collective-permute-start(bf16[512,256]{1,0:T(8,128)(2,1)} %get-tuple-element.68), channel_id=1, source_target_pairs={{0,4},{2,6},{4,0},{6,2},{1,5},{3,7},{5,1},{7,3},{8,12},{10,14},{12... | collective-permute-start | bytes 786440 | tf_op jit(solution)/shard_map/ppermute | solution.py:454
  22.7 0.0 collective-permute-done
  22.7 0.7 add.17
  23.4 8.3 %all-to-all-start = ((f32[32,8,128]{2,1,0:T(8,128)}), f32[32,8,128]{2,1,0:T(8,128)S(1)}, u32[]{:S(2)}, u32[]{:S(2)}) async-start(f32[32,8,128]{2,1,0:T(8,128)} %add.17), calls=%async_computation | async-start | bytes 262144 | tf_op jit(solution)/shard_map/all_to_all | solution.py:432
  31.6 2.9 %pick_half.1 = bf16[128,4096]{1,0:T(8,128)(2,1)} custom-call(s32[3]{0:T(128)} %pad_add_fusion.at, bf16[256,4096]{1,0:T(8,128)(2,1)} %w_own), custom_call_target="tpu_custom_call" | custom-call | bytes 2097152 | tf_op jit(solution)/shard_map/pick_half/pallas_call | solution.py:108
  34.6 0.0 collective-permute-done.1.refs_1_
  34.6 1.6 collective-permute-done.3.refs_3_
  36.2 4.5 %all-to-all-done = f32[32,8,128]{2,1,0:T(8,128)S(1)} async-done(((f32[32,8,128]{2,1,0:T(8,128)}), f32[32,8,128]{2,1,0:T(8,128)S(1)}, u32[]{:S(2)}, u32[]{:S(2)}) %all-to-all-start) | async-done | bytes 131104 | tf_op jit(solution)/shard_map/all_to_all | solution.py:432
  40.7 15.7 %all_to_all.30 = f32[64,8,128]{2,1,0:T(8,128)S(1)} all-to-all(f32[64,8,128]{2,1,0:T(8,128)S(1)} %bitcast.36), channel_id=1, replica_groups=mesh['yh'=2,'z'=8,'c'=2,'x'=4,'yl'=2] {'yh','x','yl'}, dimensions={0} | all-to-all | bytes 524288 | tf_op jit(solution)/shard_map/all_to_all | solution.py:432
  56.5 13.4 %all_to_all.31.own = f32[32,8,128]{2,1,0:T(8,128)S(1)} all-to-all(f32[32,8,128]{2,1,0:T(8,128)S(1)} %bitcast.39), channel_id=1, replica_groups=mesh['yh'=2,'z'=8,'c'=2,'x'=4,'yl'=2] {'z'}, dimensions={0} | all-to-all | bytes 262144 | tf_op jit(solution)/shard_map/all_to_all | solution.py:432
  69.9 0.4 collective-permute-start.6
  70.3 0.0 collective-permute-start.4
  70.3 1.3 collective-permute-done.4.other
  71.6 0.7 copy-done.16
  72.3 5.3 %right_part.1 = (f32[64,8,128]{2,1,0:T(8,128)}, f32[64,8,128]{2,1,0:T(8,128)}, f32[32,32]{1,0:T(8,128)}, f32[32,256]{1,0:T(8,128)}) custom-call(s32[3]{0:T(128)} %pad_add_fusion.at, f32[32,8,128]{2,1,0:T(8,128)} %copy-done.12, f32[32,8,128]{2,1,0:T(8,128)} %copy-done.16, bf16[256,2048]{1,0:T(8,128)(2,1)} %ctx.4, bf16[256,4096]{1,0:T(8,128)(2,1)} %cot.5, ...), custom_call_target="tpu_custom_call" | custom-call | flops 1610612736 | bytes 6291456 | tf_op jit(solution)/shard_map/right_part/pallas_call | solution.py:108
  77.7 0.2 collective-permute-start.5
  77.9 1.6 collective-permute-done.5
  79.5 1.7 add.18
  81.2 3.4 %all-to-all-start.3 = ((f32[64,8,128]{2,1,0:T(8,128)}), f32[64,8,128]{2,1,0:T(8,128)S(1)}, u32[]{:S(2)}, u32[]{:S(2)}) async-start(f32[64,8,128]{2,1,0:T(8,128)} %add.18), calls=%async_computation.3 | async-start | bytes 524288 | tf_op jit(solution)/shard_map/all_to_all | solution.py:432
  84.6 0.0 all-gather.5.cloned.1.call-done
  84.6 7.2 %grad_chunk.2 = (bf16[256,2560]{1,0:T(8,128)(2,1)}, bf16[256,2560]{1,0:T(8,128)(2,1)}) custom-call(s32[3]{0:T(128)} %pad_add_fusion.at, bf16[512,256]{1,0:T(8,128)(2,1)} %get-tuple-element.80.refs_0_, bf16[512,256]{1,0:T(8,128)(2,1)} %copy-done.3, bf16[512,256]{1,0:T(8,128)(2,1)} %copy-done.4, bf16[512,256]{1,0:T(8,128)(2,1)} %copy-done.5, ...), custom_call_target="tpu_custom_call" | custom-call | flops 2684354560 | bytes 10485760 | tf_op jit(solution)/shard_map/grad_chunk/pallas_call | solution.py:108
  91.8 5.2 %all-to-all-done.3 = f32[64,8,128]{2,1,0:T(8,128)S(1)} async-done(((f32[64,8,128]{2,1,0:T(8,128)}), f32[64,8,128]{2,1,0:T(8,128)S(1)}, u32[]{:S(2)}, u32[]{:S(2)}) %all-to-all-start.3) | async-done | bytes 262176 | tf_op jit(solution)/shard_map/all_to_all | solution.py:432
  97.0 0.0 collective-permute-done.6.w_half
  97.0 1.6 collective-permute-start.7
  98.6 0.0 collective-permute-start.8
  98.6 0.1 copy.9
  98.7 2.9 %cholesky.17 = f32[32,32]{1,0:T(8,128)S(1)} custom-call(f32[32,32]{1,0:T(8,128)S(1)} %fusion.3), custom_call_target="Cholesky" | custom-call | tf_op jit(solution)/shard_map/jit(cholesky)/cholesky | solution.py:476
  101.7 0.8 broadcast_in_dim.14
  102.5 6.4 %all-to-all-start.4 = ((f32[128,8,128]{2,1,0:T(8,128)}), f32[128,8,128]{2,1,0:T(8,128)S(1)}, u32[]{:S(2)}, u32[]{:S(2)}) async-start(f32[128,8,128]{2,1,0:T(8,128)} %bitcast.11), calls=%async_computation.4 | async-start | bytes 1048576 | tf_op jit(solution)/shard_map/all_to_all | solution.py:432
  108.9 0.7 compare_reduce_fusion
  109.6 0.6 fusion
  110.3 2.4 %custom-call.6 = f32[1,32,32]{1,2,0:T(8,128)S(1)} custom-call(f32[1,32,32]{2,1,0:T(8,128)S(1)} %fusion), custom_call_target="InvertDiagBlocksLowerTriangular" | custom-call | tf_op jit(solution)/shard_map/triangular_solve | solution.py:477
  112.7 0.8 fusion.1.inv
  113.5 21.8 %all-to-all-done.4 = f32[128,8,128]{2,1,0:T(8,128)S(1)} async-done(((f32[128,8,128]{2,1,0:T(8,128)}), f32[128,8,128]{2,1,0:T(8,128)S(1)}, u32[]{:S(2)}, u32[]{:S(2)}) %all-to-all-start.4) | async-done | bytes 524320 | tf_op jit(solution)/shard_map/all_to_all | solution.py:432
  135.3 0.0 collective-permute-done.8.w_other
  135.4 0.8 broadcast_in_dim.15
  136.2 3.4 %all-to-all-start.5 = ((f32[64,8,128]{2,1,0:T(8,128)}), f32[64,8,128]{2,1,0:T(8,128)S(1)}, u32[]{:S(2)}, u32[]{:S(2)}) async-start(f32[64,8,128]{2,1,0:T(8,128)} %bitcast.16), calls=%async_computation.5 | async-start | bytes 524288 | tf_op jit(solution)/shard_map/all_to_all | solution.py:432
  139.6 0.0 all-gather.7.cloned.1.call-done
  139.6 5.5 %grad_chunk.3 = (bf16[256,1536]{1,0:T(8,128)(2,1)}, bf16[256,1536]{1,0:T(8,128)(2,1)}) custom-call(s32[3]{0:T(128)} %pad_add_fusion.at, bf16[512,256]{1,0:T(8,128)(2,1)} %get-tuple-element.80.refs_0_, bf16[512,256]{1,0:T(8,128)(2,1)} %copy-done.3, bf16[512,256]{1,0:T(8,128)(2,1)} %copy-done.4, bf16[512,256]{1,0:T(8,128)(2,1)} %copy-done.5, ...), custom_call_target="tpu_custom_call" | custom-call | flops 1610612736 | bytes 6291456 | tf_op jit(solution)/shard_map/grad_chunk/pallas_call | solution.py:108
  145.1 5.2 %all-to-all-done.5.own = f32[64,8,128]{2,1,0:T(8,128)S(1)} async-done(((f32[64,8,128]{2,1,0:T(8,128)}), f32[64,8,128]{2,1,0:T(8,128)S(1)}, u32[]{:S(2)}, u32[]{:S(2)}) %all-to-all-start.5) | async-done | bytes 262176 | tf_op jit(solution)/shard_map/all_to_all | solution.py:432
  150.4 0.5 collective-permute-start.9
  150.9 8.5 %ctx_blocks.1 = (bf16[256,512]{1,0:T(8,128)(2,1)}, bf16[256,512]{1,0:T(8,128)(2,1)}, bf16[256,512]{1,0:T(8,128)(2,1)}, bf16[256,512]{1,0:T(8,128)(2,1)}) custom-call(s32[3]{0:T(128)} %pad_add_fusion.at, bf16[256,4096]{1,0:T(8,128)(2,1)} %cot.5, bf16[256,4096]{1,0:T(8,128)(2,1)} %w_own, bf16[128,4096]{1,0:T(8,128)(2,1)} %copy-done.14, ...), custom_call_target="tpu_custom_call" | custom-call | flops 4294967296 | bytes 16777216 | tf_op jit(solution)/shard_map/ctx_blocks/pallas_call | solution.py:108
  159.3 0.0 collective-permute-done.10.other
  159.4 7.5 %collective-permute-done.9.refs_3_ = bf16[256,1536]{1,0:T(8,128)(2,1)S(1)} collective-permute-done((bf16[256,1536]{1,0:T(8,128)(2,1)}, bf16[256,1536]{1,0:T(8,128)(2,1)S(1)}, u32[]{:S(2)}, u32[]{:S(2)}) %collective-permute-start.9) | collective-permute-done | bytes 786464 | tf_op jit(solution)/shard_map/ppermute | solution.py:486
  166.9 1.1 collective-permute-start.11
  168.0 0.9 collective-permute-start.12
  168.9 2.2 %collective-permute-start.13 = (bf16[256,512]{1,0:T(8,128)(2,1)}, bf16[256,512]{1,0:T(8,128)(2,1)S(1)}, u32[]{:S(2)}, u32[]{:S(2)}) collective-permute-start(bf16[256,512]{1,0:T(8,128)(2,1)} %get-tuple-element.105), channel_id=1, source_target_pairs={{0,4},{2,6},{4,0},{6,2},{1,5},{3,7},{5,1},{7,3},{8,12},{10,14},{12... | collective-permute-start | bytes 786440 | tf_op jit(solution)/shard_map/ppermute | solution.py:492
  171.1 7.4 %final_part.1 = (f32[32,4096]{1,0:T(8,128)}, bf16[256,4096]{1,0:T(8,128)(2,1)}, bf16[256,4096]{1,0:T(8,128)(2,1)}) custom-call(s32[3]{0:T(128)} %pad_add_fusion.at, f32[32,32]{1,0:T(8,128)} %fusion.1.inv, f32[32,256]{1,0:T(8,128)} %get-tuple-element.107.rows, f32[64,8,128]{2,1,0:T(8,128)} %copy-done.2, f32[64,8,128]{2,1,0:T(8,128)} %copy-done.7, ...), custom_call_target="tpu_custom_call" | custom-call | flops 536870912 | bytes 8388608 | tf_op jit(solution)/shard_map/final_part/pallas_call | solution.py:108
  178.5 0.0 collective-permute-done.12.refs_2_
  178.5 1.2 collective-permute-done.13.refs_3_
  179.7 0.7 copy-done.10
  180.4 2.9 %place.1 = bf16[256,2048]{1,0:T(8,128)(2,1)} custom-call(s32[3]{0:T(128)} %pad_add_fusion.at, bf16[256,512]{1,0:T(8,128)(2,1)} %get-tuple-element.102.refs_0_, bf16[256,512]{1,0:T(8,128)(2,1)} %copy-done.8, bf16[256,512]{1,0:T(8,128)(2,1)} %copy-done.9, bf16[256,512]{1,0:T(8,128)(2,1)} %copy-done.10), custom_call_target="tpu_custom_call" | custom-call | bytes 2097152 | tf_op jit(solution)/shard_map/place/pallas_call | solution.py:108
  (44 shorter events, 0.2 us)
Async XLA Ops:
  7.2 77.5 %all-gather.5.cloned.1.call-start = ((), (), s32[]{:S(2)}) async-start(), calls=%async_computation.6 | async-start | bytes 6553600 | tf_op jit(solution)/shard_map/all_gather | solution.py:449
  7.9 5.0 %copy-start = (bf16[256,4096]{1,0:T(8,128)(2,1)S(1)}, bf16[256,4096]{1,0:T(8,128)(2,1)}, u32[]{:S(2)}) copy-start(bf16[256,4096]{1,0:T(8,128)(2,1)} %cot.5) | copy-start | bytes 6291460
  14.1 1.0 copy-start.15
  14.1 8.6 %copy-start.11 = (f32[32,8,128]{2,1,0:T(8,128)S(1)}, f32[32,8,128]{2,1,0:T(8,128)}, u32[]{:S(2)}) copy-start(f32[32,8,128]{2,1,0:T(8,128)} %get-tuple-element.62) | copy-start | bytes 393220
  14.1 125.5 %all-gather.7.cloned.1.call-start = ((), (), s32[]{:S(2)}) async-start(), calls=%async_computation.7 | async-start | bytes 3932160 | tf_op jit(solution)/shard_map/all_gather | solution.py:449
  15.1 7.5 %collective-permute-start = (f32[32,8,128]{2,1,0:T(8,128)S(1)}, f32[32,8,128]{2,1,0:T(8,128)S(1)}, u32[]{:S(2)}, u32[]{:S(2)}) collective-permute-start(f32[32,8,128]{2,1,0:T(8,128)S(1)} %copy-done.15), channel_id=1, source_target_pairs={{0,8},{8,0},{1,9},{9,1},{2,10},{10,2},{3,11},{11,3},{4,12},{12,4},... | collective-permute-start | bytes 393224 | tf_op jit(solution)/shard_map/ppermute | solution.py:455
  18.2 16.3 %collective-permute-start.1 = (bf16[512,256]{1,0:T(8,128)(2,1)}, bf16[512,256]{1,0:T(8,128)(2,1)S(1)}, u32[]{:S(2)}, u32[]{:S(2)}) collective-permute-start(bf16[512,256]{1,0:T(8,128)(2,1)} %get-tuple-element.66), channel_id=1, source_target_pairs={{0,2},{2,4},{4,6},{6,0},{1,3},{3,5},{5,7},{7,1},{8,10},{10,12},{12... | collective-permute-start | bytes 786440 | tf_op jit(solution)/shard_map/ppermute | solution.py:454
  19.8 14.8 %collective-permute-start.2 = (bf16[512,256]{1,0:T(8,128)(2,1)}, bf16[512,256]{1,0:T(8,128)(2,1)S(1)}, u32[]{:S(2)}, u32[]{:S(2)}) collective-permute-start(bf16[512,256]{1,0:T(8,128)(2,1)} %get-tuple-element.67), channel_id=1, source_target_pairs={{2,0},{4,2},{6,4},{0,6},{3,1},{5,3},{7,5},{1,7},{10,8},{12,10},{14... | collective-permute-start | bytes 786440 | tf_op jit(solution)/shard_map/ppermute | solution.py:454
  20.7 15.6 %collective-permute-start.3 = (bf16[512,256]{1,0:T(8,128)(2,1)}, bf16[512,256]{1,0:T(8,128)(2,1)S(1)}, u32[]{:S(2)}, u32[]{:S(2)}) collective-permute-start(bf16[512,256]{1,0:T(8,128)(2,1)} %get-tuple-element.68), channel_id=1, source_target_pairs={{0,4},{2,6},{4,0},{6,2},{1,5},{3,7},{5,1},{7,3},{8,12},{10,14},{12... | collective-permute-start | bytes 786440 | tf_op jit(solution)/shard_map/ppermute | solution.py:454
  23.4 17.4 %all-to-all-start = ((f32[32,8,128]{2,1,0:T(8,128)}), f32[32,8,128]{2,1,0:T(8,128)S(1)}, u32[]{:S(2)}, u32[]{:S(2)}) async-start(f32[32,8,128]{2,1,0:T(8,128)} %add.17), calls=%async_computation | async-start | bytes 262144 | tf_op jit(solution)/shard_map/all_to_all | solution.py:432
  34.6 43.0 %copy-start.3 = (bf16[512,256]{1,0:T(8,128)(2,1)}, bf16[512,256]{1,0:T(8,128)(2,1)S(1)}, u32[]{:S(2)}) copy-start(bf16[512,256]{1,0:T(8,128)(2,1)S(1)} %collective-permute-done.1.refs_1_) | copy-start | bytes 786436
  34.6 43.0 %copy-start.4 = (bf16[512,256]{1,0:T(8,128)(2,1)}, bf16[512,256]{1,0:T(8,128)(2,1)S(1)}, u32[]{:S(2)}) copy-start(bf16[512,256]{1,0:T(8,128)(2,1)S(1)} %collective-permute-done.2.refs_2_) | copy-start | bytes 786436
  36.2 41.4 %copy-start.5 = (bf16[512,256]{1,0:T(8,128)(2,1)}, bf16[512,256]{1,0:T(8,128)(2,1)S(1)}, u32[]{:S(2)}) copy-start(bf16[512,256]{1,0:T(8,128)(2,1)S(1)} %collective-permute-done.3.refs_3_) | copy-start | bytes 786436
  69.9 1.7 copy-start.12
  69.9 27.1 %collective-permute-start.6 = (bf16[128,4096]{1,0:T(8,128)(2,1)}, bf16[128,4096]{1,0:T(8,128)(2,1)S(1)}, u32[]{:S(2)}, u32[]{:S(2)}) collective-permute-start(bf16[128,4096]{1,0:T(8,128)(2,1)} %pick_half.1), channel_id=1, source_target_pairs={{0,1},{1,0},{2,3},{3,2},{4,5},{5,4},{6,7},{7,6},{8,9},{9,8},{10,11... | collective-permute-start | bytes 3145736 | tf_op jit(solution)/shard_map/ppermute | solution.py:464
  70.3 1.3 collective-permute-start.4
  71.6 0.7 copy-start.16
  77.7 1.8 collective-permute-start.5
  81.2 15.8 %all-to-all-start.3 = ((f32[64,8,128]{2,1,0:T(8,128)}), f32[64,8,128]{2,1,0:T(8,128)S(1)}, u32[]{:S(2)}, u32[]{:S(2)}) async-start(f32[64,8,128]{2,1,0:T(8,128)} %add.18), calls=%async_computation.3 | async-start | bytes 524288 | tf_op jit(solution)/shard_map/all_to_all | solution.py:432
  84.6 14.0 %copy-start.13 = (f32[32,32]{1,0:T(8,128)S(1)}, f32[32,32]{1,0:T(8,128)}, u32[]{:S(2)}) copy-start(f32[32,32]{1,0:T(8,128)} %get-tuple-element.90) | copy-start | bytes 12292
  97.0 53.9 %copy-start.14 = (bf16[128,4096]{1,0:T(8,128)(2,1)}, bf16[128,4096]{1,0:T(8,128)(2,1)S(1)}, u32[]{:S(2)}) copy-start(bf16[128,4096]{1,0:T(8,128)(2,1)S(1)} %collective-permute-done.6.w_half) | copy-start | bytes 3145732
  97.0 38.3 %collective-permute-start.7 = (bf16[256,2560]{1,0:T(8,128)(2,1)}, bf16[256,2560]{1,0:T(8,128)(2,1)S(1)}, u32[]{:S(2)}, u32[]{:S(2)}) collective-permute-start(bf16[256,2560]{1,0:T(8,128)(2,1)} %get-tuple-element.89), channel_id=1, source_target_pairs={{0,1},{1,0},{2,3},{3,2},{4,5},{5,4},{6,7},{7,6},{8,9},{9,8},{10,11... | collective-permute-start | bytes 3932168 | tf_op jit(solution)/shard_map/ppermute | solution.py:473
  98.6 36.7 %collective-permute-start.8 = (bf16[128,4096]{1,0:T(8,128)(2,1)S(1)}, bf16[128,4096]{1,0:T(8,128)(2,1)}, u32[]{:S(2)}, u32[]{:S(2)}) collective-permute-start(bf16[128,4096]{1,0:T(8,128)(2,1)S(1)} %collective-permute-done.6.w_half), channel_id=1, source_target_pairs={{0,8},{8,0},{1,9},{9,1},{2,10},{10,2},{3,11},{11,3},{4,12},{12,4},... | collective-permute-start | bytes 3145736 | tf_op jit(solution)/shard_map/ppermute | solution.py:474
  102.5 32.8 %all-to-all-start.4 = ((f32[128,8,128]{2,1,0:T(8,128)}), f32[128,8,128]{2,1,0:T(8,128)S(1)}, u32[]{:S(2)}, u32[]{:S(2)}) async-start(f32[128,8,128]{2,1,0:T(8,128)} %bitcast.11), calls=%async_computation.4 | async-start | bytes 1048576 | tf_op jit(solution)/shard_map/all_to_all | solution.py:432
  135.3 9.8 %copy-start.1 = (bf16[256,2560]{1,0:T(8,128)(2,1)}, bf16[256,2560]{1,0:T(8,128)(2,1)S(1)}, u32[]{:S(2)}) copy-start(bf16[256,2560]{1,0:T(8,128)(2,1)S(1)} %collective-permute-done.7.refs_2_) | copy-start | bytes 3932164
  136.2 14.2 %all-to-all-start.5 = ((f32[64,8,128]{2,1,0:T(8,128)}), f32[64,8,128]{2,1,0:T(8,128)S(1)}, u32[]{:S(2)}, u32[]{:S(2)}) async-start(f32[64,8,128]{2,1,0:T(8,128)} %bitcast.16), calls=%async_computation.5 | async-start | bytes 524288 | tf_op jit(solution)/shard_map/all_to_all | solution.py:432
  150.4 9.0 %copy-start.2 = (f32[64,8,128]{2,1,0:T(8,128)}, f32[64,8,128]{2,1,0:T(8,128)S(1)}, u32[]{:S(2)}) copy-start(f32[64,8,128]{2,1,0:T(8,128)S(1)} %all-to-all-done.5.own) | copy-start | bytes 786436
  150.4 16.5 %collective-permute-start.9 = (bf16[256,1536]{1,0:T(8,128)(2,1)}, bf16[256,1536]{1,0:T(8,128)(2,1)S(1)}, u32[]{:S(2)}, u32[]{:S(2)}) collective-permute-start(bf16[256,1536]{1,0:T(8,128)(2,1)} %get-tuple-element.95), channel_id=1, source_target_pairs={{0,1},{1,0},{2,3},{3,2},{4,5},{5,4},{6,7},{7,6},{8,9},{9,8},{10,11... | collective-permute-start | bytes 2359304 | tf_op jit(solution)/shard_map/ppermute | solution.py:486
  150.9 8.5 %collective-permute-start.10 = (f32[64,8,128]{2,1,0:T(8,128)S(1)}, f32[64,8,128]{2,1,0:T(8,128)S(1)}, u32[]{:S(2)}, u32[]{:S(2)}) collective-permute-start(f32[64,8,128]{2,1,0:T(8,128)S(1)} %all-to-all-done.5.own), channel_id=1, source_target_pairs={{0,8},{8,0},{1,9},{9,1},{2,10},{10,2},{3,11},{11,3},{4,12},{12,4},... | collective-permute-start | bytes 786440 | tf_op jit(solution)/shard_map/ppermute | solution.py:487
  159.4 11.8 %copy-start.7 = (f32[64,8,128]{2,1,0:T(8,128)}, f32[64,8,128]{2,1,0:T(8,128)S(1)}, u32[]{:S(2)}) copy-start(f32[64,8,128]{2,1,0:T(8,128)S(1)} %collective-permute-done.10.other) | copy-start | bytes 786436
  166.9 4.2 %copy-start.6 = (bf16[256,1536]{1,0:T(8,128)(2,1)}, bf16[256,1536]{1,0:T(8,128)(2,1)S(1)}, u32[]{:S(2)}) copy-start(bf16[256,1536]{1,0:T(8,128)(2,1)S(1)} %collective-permute-done.9.refs_3_) | copy-start | bytes 2359300
  166.9 11.6 %collective-permute-start.11 = (bf16[256,512]{1,0:T(8,128)(2,1)}, bf16[256,512]{1,0:T(8,128)(2,1)S(1)}, u32[]{:S(2)}, u32[]{:S(2)}) collective-permute-start(bf16[256,512]{1,0:T(8,128)(2,1)} %get-tuple-element.103), channel_id=1, source_target_pairs={{0,2},{2,4},{4,6},{6,0},{1,3},{3,5},{5,7},{7,1},{8,10},{10,12},{12... | collective-permute-start | bytes 786440 | tf_op jit(solution)/shard_map/ppermute | solution.py:492
  168.0 10.5 %collective-permute-start.12 = (bf16[256,512]{1,0:T(8,128)(2,1)}, bf16[256,512]{1,0:T(8,128)(2,1)S(1)}, u32[]{:S(2)}, u32[]{:S(2)}) collective-permute-start(bf16[256,512]{1,0:T(8,128)(2,1)} %get-tuple-element.104), channel_id=1, source_target_pairs={{2,0},{4,2},{6,4},{0,6},{3,1},{5,3},{7,5},{1,7},{10,8},{12,10},{14... | collective-permute-start | bytes 786440 | tf_op jit(solution)/shard_map/ppermute | solution.py:492
  168.9 10.8 %collective-permute-start.13 = (bf16[256,512]{1,0:T(8,128)(2,1)}, bf16[256,512]{1,0:T(8,128)(2,1)S(1)}, u32[]{:S(2)}, u32[]{:S(2)}) collective-permute-start(bf16[256,512]{1,0:T(8,128)(2,1)} %get-tuple-element.105), channel_id=1, source_target_pairs={{0,4},{2,6},{4,0},{6,2},{1,5},{3,7},{5,1},{7,3},{8,12},{10,14},{12... | collective-permute-start | bytes 786440 | tf_op jit(solution)/shard_map/ppermute | solution.py:492
  178.5 1.2 copy-start.8
  178.5 1.2 copy-start.9
  179.7 0.7 copy-start.10
Sparse Core Ops, SparseCore 0:
  14.2 66.2 all-gather.4
  82.9 48.6 all-gather.6

commit v2 on v1

--- a/solution.py
+++ b/solution.py
@@ -20,8 +20,8 @@
 DIM = 4096
 RANK = 32
 N_REP = 32
-SPLIT = (2560, 1536)
-STARTS = (0, 2560)
+SPLIT = (1536, 1536, 1024)
+STARTS = (0, 1536, 3072)
 TILE = 512
 FTILE = 512
 VMEM = 60 << 20
@@ -103,7 +103,7 @@
         copy.wait()
 
 
-def call(kernel, name, ins, outs, scratch, flops, size, alias=None):
+def call(kernel, name, ins, outs, scratch, flops, size, alias=None, hide=False):
     spec = lambda inside: pl.BlockSpec(memory_space=pltpu.VMEM if inside else pl.ANY)
     return pl.pallas_call(
         kernel,
@@ -113,7 +113,7 @@
         scratch_shapes=scratch,
         input_output_aliases=alias or {},
         compiler_params=params(),
-        cost_estimate=cost(flops, size),
+        cost_estimate=cost(flops, size) if hide else cost(1, 1),
         name=name,
     )(*[a for a, _ in ins])
 
@@ -246,36 +246,18 @@
     return call(pick_kernel, "pick_half", [(at, True), (a, False)], outs, [DMA(4)], 0, 2 << 20)[0]
 
 
-def place_kernel(at, *refs):
-    parts, dst, sems = refs[:4], refs[4], refs[5]
-    width = parts[0].shape[1]
-    pairs = []
-    for part, k in zip(parts, (0, 3, 1, 2)):
-        lane = pl.multiple_of(lax.rem(at[0] + k, 4) * width, width)
-        pairs.append((part, dst.at[:, pl.ds(lane, width)]))
-    wait(copies(sems, pairs))
-
-
-def place(at, parts):
-    tok, width = parts[0].shape
-    ins = [(at, True)] + [(a, False) for a in parts]
-    outs = [((tok, 4 * width), BF16, True)]
-    return call(place_kernel, "place", ins, outs, [DMA(4)], 0, 2 << 20)[0]
-
-
-def block_pairs(at, start, j, cot, others, buf, tile=None):
-    here = pl.ds(j * TILE, TILE)
-    tile = j if tile is None else tile
-    pairs = [(cot.at[:, pl.ds(start + j * TILE, TILE)], buf.at[tile, pl.ds(0, TOK)])]
+def block_pairs(at, col, cot, wide, buf):
+    cols = pl.ds(col, TILE)
+    pairs = [(cot.at[:, cols], buf.at[pl.ds(0, TOK)])]
     for i, k in enumerate((3, 1, 2)):
-        src = others[0].at[lax.rem(at[0] + k, 4), :, here] if len(others) == 1 else others[i].at[:, here]
-        pairs.append((src, buf.at[tile, pl.ds((i + 1) * TOK, TOK)]))
+        src = wide.at[lax.rem(at[0] + k, 4), :, cols]
+        pairs.append((src, buf.at[pl.ds((i + 1) * TOK, TOK)]))
     return pairs
 
 
-def grad_kernel(start, count, n, at, *refs):
-    ctx, cot, err, others = refs[:4], refs[4], refs[5], refs[6 : 6 + n]
-    kept, sent, lhs, buf, err_v, out_k, out_s, in_sems, out_sems = refs[-9:]
+def grad_kernel(start, count, at, *refs):
+    ctx, cot, err, wide, kept, sent = refs[:4], *refs[4:9]
+    lhs, buf, err_v, out_k, out_s, in_sems, out_sems = refs[9:]
     yl = at[1]
     pairs = []
     for k, block in enumerate(ctx):
@@ -284,8 +266,9 @@
             to = lhs.at[pl.ds(i * ROWS, ROWS), pl.ds(k * TOK, TOK)]
             pairs.append((block.at[rows, :], to))
     for j in range(count):
-        pairs += block_pairs(at, start, j, cot, others, buf)
-        pairs.append((err.at[:, pl.ds(start + j * TILE, TILE)], err_v.at[j]))
+        col = start + j * TILE
+        pairs += block_pairs(at, col, cot, wide, buf.at[j])
+        pairs.append((err.at[:, pl.ds(col, TILE)], err_v.at[j]))
     started = copies(in_sems, pairs)
     wait(started[:8])
     done = []
@@ -294,24 +277,21 @@
         out = dot(lhs[...], buf[j], NN)
         out_k[j] = (out[:ROWS] + err_v[j].astype(F32)).astype(BF16)
         out_s[j] = out[ROWS:].astype(BF16)
+        here = pl.ds(j * TILE, TILE)
         done += copies(
             out_sems.at[pl.ds(2 * j, 2)],
-            [
-                (out_k.at[j], kept.at[:, pl.ds(j * TILE, TILE)]),
-                (out_s.at[j], sent.at[:, pl.ds(j * TILE, TILE)]),
-            ],
+            [(out_k.at[j], kept.at[:, here]), (out_s.at[j], sent.at[:, here])],
         )
     wait(done)
 
 
-def grad_chunk(at, ctx, cot, err, others, start):
-    width = others[0].shape[-1]
+def grad_chunk(at, ctx, cot, err, wide, start, width):
     count = width // TILE
     return call(
-        functools.partial(grad_kernel, start, count, len(others)),
+        functools.partial(grad_kernel, start, count),
         "grad_chunk",
-        [(at, True)] + [(a, False) for a in (*ctx, cot, err, *others)],
-        [((ROWS, width), BF16, False), ((ROWS, width), BF16, False)],
+        [(at, True)] + [(a, False) for a in (*ctx, cot, err, wide)],
+        [((ROWS, width), BF16, False)] * 2,
         [
             pltpu.VMEM((2 * ROWS, 4 * TOK), BF16),
             pltpu.VMEM((count, 4 * TOK, TILE), BF16),
@@ -323,24 +303,22 @@
         ],
         2 * 512 * 1024 * width,
         4 * 1024 * width,
-    )
-
-
-def ctx_kernel(sizes, at, cot, w_own, w_half, w_other, *refs):
-    outs, (buf, wbuf, acc, sems) = refs[-8:-4], refs[-4:]
+        hide=True,
+    )
+
+
+def ctx_kernel(at, cot, w_own, w_half, w_other, wide, *refs):
+    outs, (buf, wbuf, acc, sems) = refs[:4], refs[4:]
+    half = ROWS // 2
+    count = DIM // TILE
     pairs = []
-    tile = 0
-    for n, start, width in sizes:
-        others, refs = refs[:n], refs[n:]
-        for j in range(width // TILE):
-            pairs += block_pairs(at, start, j, cot, others, buf, tile)
-            cols = pl.ds(start + j * TILE, TILE)
-            half = ROWS // 2
-            for w, row, m in ((w_own, 0, ROWS), (w_half, ROWS, half), (w_other, ROWS + half, half)):
-                pairs.append((w.at[:, cols], wbuf.at[tile, pl.ds(row, m)]))
-            tile += 1
+    for j in range(count):
+        pairs += block_pairs(at, j * TILE, cot, wide, buf.at[j])
+        cols = pl.ds(j * TILE, TILE)
+        for w, row, m in ((w_own, 0, ROWS), (w_half, ROWS, half), (w_other, ROWS + half, half)):
+            pairs.append((w.at[:, cols], wbuf.at[j, pl.ds(row, m)]))
     started = copies(sems, pairs)
-    for j in range(tile):
+    for j in range(count):
         wait(started[7 * j : 7 * j + 7])
         part = dot(buf[j], wbuf[j], NT)
         if j == 0:
@@ -348,7 +326,6 @@
         else:
             acc[...] += part
     yl, c = at[1], at[2]
-    half = ROWS // 2
     mine = pl.ds(pl.multiple_of(yl * ROWS, ROWS), ROWS)
     for k, out in enumerate(outs):
         tok = slice(k * TOK, (k + 1) * TOK)
@@ -360,14 +337,12 @@
             )
 
 
-def ctx_blocks(at, cot, groups, weights):
-    sizes = [(len(others), start, others[0].shape[-1]) for start, others in groups]
+def ctx_blocks(at, cot, wide, weights):
     count = DIM // TILE
-    flat = [a for _, others in groups for a in others]
-    return call(
-        functools.partial(ctx_kernel, sizes),
+    return call(
+        ctx_kernel,
         "ctx_blocks",
-        [(at, True)] + [(a, False) for a in (cot, *weights, *flat)],
+        [(at, True)] + [(a, False) for a in (cot, *weights, wide)],
         [((TOK, 2 * ROWS), BF16, True)] * 4,
         [
             pltpu.VMEM((count, 4 * TOK, TILE), BF16),
@@ -381,49 +356,99 @@
 
 
 def final_kernel(at, inv, rows, own, other, *refs):
-    n = len(SPLIT)
-    kept, got = refs[:n], refs[n : 2 * n]
-    basis, update, new_err, q, kept_v, got_v, up_v, new_v, in_sems, out_sems = refs[2 * n :]
-    sides = [slice(j * FTILE, (j + 1) * FTILE) for j in range(DIM // FTILE)]
+    kept, got, refs = refs[:2], refs[2:4], refs[4:]
+    basis, pb, update, new_err, q, nb6, kept_v, got_v, up_v, new_v = refs[:10]
+    in_sems, up_sems, new_sems = refs[10:]
+    sides = [pl.ds(j * FTILE, FTILE) for j in range(DIM // FTILE)]
+    known = STARTS[2] // FTILE
     pairs = []
-    for j, s in enumerate(sides):
-        i = max(i for i in range(n) if STARTS[i] <= s.start)
-        src = pl.ds(s.start - STARTS[i], FTILE)
+    for j in range(known):
+        i = 1 if j * FTILE >= STARTS[1] else 0
+        src = pl.ds(j * FTILE - STARTS[i], FTILE)
         pairs += [(kept[i].at[:, src], kept_v.at[j]), (got[i].at[:, src], got_v.at[j])]
     started = copies(in_sems, pairs)
     from_tiles(own, at[2] * 16, q)
     from_tiles(other, (1 - at[2]) * 16, q)
     inv6 = left6(inv[...].T)
-    pb = left6(dot(inv6, right6(rows[...]), TN))
+    pb[...] = left6(dot(inv6, right6(rows[...]), TN))
+    nb = dot(inv6, right6(q[...]), TN) * (1.0 / N_REP)
+    basis[...] = nb
+    nb6[...] = right6(nb)
     done = []
     for j, s in enumerate(sides):
-        nb = dot(inv6, right6(q[:, s]), TN) * (1.0 / N_REP)
-        basis[:, s] = nb
-        low = dot(pb, right6(nb), TN)
+        low = dot(pb[...], nb6[:, s], TN)
         up_v[j] = low.astype(BF16)
-        wait(started[2 * j : 2 * j + 2])
-        new_v[j] = (kept_v[j].astype(F32) + got_v[j].astype(F32) - low).astype(BF16)
-        here = pl.ds(s.start, FTILE)
-        done += copies(
-            out_sems.at[pl.ds(2 * j, 2)],
-            [(up_v.at[j], update.at[:, here]), (new_v.at[j], new_err.at[:, here])],
-        )
+        done += copies(up_sems.at[pl.ds(j, 1)], [(up_v.at[j], update.at[:, s])])
+        if j < known:
+            wait(started[2 * j : 2 * j + 2])
+            new_v[j] = (kept_v[j].astype(F32) + got_v[j].astype(F32) - low).astype(BF16)
+            done += copies(new_sems.at[pl.ds(j, 1)], [(new_v.at[j], new_err.at[:, s])])
     wait(done)
 
 
 def final_part(at, inv, rows, own, other, kept, got):
-    n = DIM // FTILE
+    n, known = DIM // FTILE, STARTS[2] // FTILE
+    wide = lambda k: pltpu.VMEM((k, ROWS, FTILE), BF16)
     return call(
         final_kernel,
         "final_part",
         [(at, True), (inv, True), (rows, True), (own, True), (other, True)]
         + [(a, False) for a in (*kept, *got)],
-        [((RANK, DIM), F32, True), ((ROWS, DIM), BF16, False), ((ROWS, DIM), BF16, False)],
-        [pltpu.VMEM((RANK, DIM), F32)]
-        + [pltpu.VMEM((n, ROWS, FTILE), BF16)] * 4
-        + [DMA(2 * n), DMA(2 * n)],
+        [
+            ((RANK, DIM), F32, True),
+            ((6 * RANK, ROWS), BF16, True),
+            ((ROWS, DIM), BF16, False),
+            ((ROWS, DIM), BF16, False),
+        ],
+        [pltpu.VMEM((RANK, DIM), F32), pltpu.VMEM((6 * RANK, DIM), BF16)]
+        + [wide(known), wide(known), wide(n), wide(known)]
+        + [DMA(2 * known), DMA(n), DMA(known)],
         2 * 256 * 256 * 4096,
         8 << 20,
+    )
+
+
+def last_kernel(at, basis, pb, kept, got, *refs):
+    parts, new_err, grad = refs[:4], refs[5], refs[6]
+    kept_v, got_v, new_v, part_v, sems, new_sems, part_sems, grad_sems = refs[7:]
+    count = SPLIT[2] // FTILE
+    pairs = []
+    for j in range(count):
+        src = pl.ds(j * FTILE, FTILE)
+        pairs += [(kept.at[:, src], kept_v.at[j]), (got.at[:, src], got_v.at[j])]
+    started = copies(sems, pairs)
+    arriving = copies(part_sems, [(part, part_v.at[i]) for i, part in enumerate(parts)])
+    done = []
+    for j in range(count):
+        s = pl.ds(STARTS[2] + j * FTILE, FTILE)
+        low = dot(pb[...], right6(basis[:, s]), TN)
+        wait(started[2 * j : 2 * j + 2])
+        new_v[j] = (kept_v[j].astype(F32) + got_v[j].astype(F32) - low).astype(BF16)
+        done += copies(new_sems.at[pl.ds(j, 1)], [(new_v.at[j], new_err.at[:, s])])
+    width = 2 * ROWS
+    for i, k in enumerate((0, 3, 1, 2)):
+        lane = pl.multiple_of(lax.rem(at[0] + k, 4) * width, width)
+        wait(arriving[i : i + 1])
+        done += copies(
+            grad_sems.at[pl.ds(i, 1)], [(part_v.at[i], grad.at[:, pl.ds(lane, width)])]
+        )
+    wait(done)
+
+
+def last_part(at, basis, pb, kept, got, parts, partial):
+    count = SPLIT[2] // FTILE
+    return call(
+        last_kernel,
+        "last_part",
+        [(at, True), (basis, True), (pb, True)]
+        + [(a, False) for a in (kept, got, *parts, partial)],
+        [((ROWS, DIM), BF16, False), ((TOK, HD), BF16, False)],
+        [pltpu.VMEM((count, ROWS, FTILE), BF16)] * 3
+        + [pltpu.VMEM((4, TOK, 2 * ROWS), BF16)]
+        + [DMA(2 * count), DMA(count), DMA(4), DMA(4)],
+        2 * 256 * 256 * 1024,
+        4 << 20,
+        {9: 0},
     )
 
 
@@ -432,9 +457,13 @@
     return lax.all_to_all(t, axes, 0, 0, tiled=True).reshape(n, -1, 8, 128)
 
 
+def copies_for(m, axes):
+    n = lax.axis_size(axes)
+    return jnp.broadcast_to(m[None], (n,) + m.shape).reshape(-1, 8, 128)
+
+
 def collect(m, axes):
-    n = lax.axis_size(axes)
-    return spread(jnp.broadcast_to(m[None], (n,) + m.shape).reshape(-1, 8, 128), axes)
+    return spread(copies_for(m, axes), axes)
 
 
 def body(context, cotangent, out_weight, error_buffer, seed_basis):
@@ -442,12 +471,10 @@
     at = jnp.stack([x, yl, c]).astype(jnp.int32)
     error = error_buffer[0]
 
+    wide = lax.all_gather(cotangent, "x", axis=0)
+
     keep, send = left_part(at, seed_basis.T, cotangent, error, context)
-    keep, send, cot, ctx, weight = fence((keep, send, cotangent, context, out_weight))
-
-    wide_a, wide_b = [
-        [lax.all_gather(cot[:, a : a + n], "x", axis=0)] for a, n in zip(STARTS, SPLIT)
-    ]
+    keep, send, ctx, weight = fence((keep, send, context, out_weight))
 
     moved = quarters(at, ctx)
     perms = (RIGHT, LEFT, OPPOSITE)
@@ -467,33 +494,39 @@
     keep, send, gram, p_rows = right_part(at, pt, po, context, cotangent, error)
     keep, send, gram = fence((keep, send, gram))
     got = spread(keep + lax.ppermute(send, "c", SWAP), "z")
-    kept_a, sent_a = grad_chunk(at, ctx_x, cotangent, error, wide_a, STARTS[0])
-    got, kept_a, sent_a, half = fence((got, kept_a, sent_a, half))
-
-    got_a = lax.ppermute(sent_a, "yl", SWAP)
-    other = lax.ppermute(half, "c", SWAP)
-    got = collect(jnp.sum(got, 0), ("yh", "x", "yl"))
     chol = jnp.linalg.cholesky(gram)
     inv = lax.linalg.triangular_solve(
         chol, jnp.eye(RANK, dtype=F32), left_side=True, lower=True
     )
-    got, got_a, inv, other = fence((got, got_a, inv, other))
-
-    qt = collect(jnp.sum(got, 0), "z").reshape(-1, 8, 128)
-    kept_b, sent_b = grad_chunk(at, ctx_x, cotangent, error, wide_b, STARTS[1])
-    qt, kept_b, sent_b = fence((qt, kept_b, sent_b))
-
+    got, inv, half = fence((got, inv, half))
+
+    other = lax.ppermute(half, "c", SWAP)
+    got = collect(jnp.sum(got, 0), ("yh", "x", "yl"))
+    grad = lambda i: grad_chunk(at, ctx_x, cotangent, error, wide, STARTS[i], SPLIT[i])
+    kept_a, sent_a = grad(0)
+    got, other, kept_a, sent_a = fence((got, other, kept_a, sent_a))
+
+    got_a = lax.ppermute(sent_a, "yl", SWAP)
+    out, late = fence((copies_for(jnp.sum(got, 0), "z"), wide))
+    qt = spread(out, "z").reshape(-1, 8, 128)
+    grad = lambda i: grad_chunk(at, ctx_x, cotangent, error, late, STARTS[i], SPLIT[i])
+    kept_b, sent_b = grad(1)
     got_b = lax.ppermute(sent_b, "yl", SWAP)
+    kept_c, sent_c = grad(2)
+    qt, kept_b, kept_c, sent_c = fence((qt, kept_b, kept_c, sent_c))
+
+    got_c = lax.ppermute(sent_c, "yl", SWAP)
     qo = lax.ppermute(qt, "c", SWAP)
-    groups = list(zip(STARTS, (wide_a, wide_b)))
-    blocks = ctx_blocks(at, cotangent, groups, [weight, half, other])
-    got_b, qo, blocks = fence((got_b, qo, blocks))
+    blocks = ctx_blocks(at, cotangent, wide, [weight, half, other])
+    qo, blocks = fence((qo, blocks))
     back = (LEFT, RIGHT, OPPOSITE)
     home = [blocks[0]] + [lax.ppermute(m, "x", p) for m, p in zip(blocks[1:], back)]
-    new_basis, update, new_error = final_part(
+    new_basis, pb, update, partial = final_part(
         at, inv, p_rows, qt, qo, (kept_a, kept_b), (got_a, got_b)
     )
-    ctx_grad = place(at, [home[0], home[2], home[1], home[3]])
+    new_basis, got_c, home, partial = fence((new_basis, got_c, home, partial))
+    parts = [home[0], home[2], home[1], home[3]]
+    new_error, ctx_grad = last_part(at, new_basis, pb, kept_c, got_c, parts, partial)
     return (ctx_grad, update, new_error[None], new_basis.T)
 
 

time: 192 us -> 177 us (0.922)
  waiting for transfers between devices: 50 us -> 27.9 us
  Pallas kernels: 47.6 us -> 50.2 us
  starting transfers between devices: 33.1 us -> 35.4 us
    all_to_all x4, waiting for transfers between devices: 36.7 us -> 16 us  [spread(): return lax.all_to_all(t, axes, 0, 0, tiled=True).reshape(n, -1, 8, 128)]
    pallas_call x9 -> x10, Pallas kernels: 47.6 us -> 50.2 us  [call(): pl.pallas_call(kernel, in_specs=[pl.BlockSpec(memory_space=pltpu.SMEM)] +...]
    slice x2 -> x0, local copies, waits for them, and re-layouts: 2.09 us -> none  [body(): cot[:, a:a + n]]
  transfers between devices with their start and end apart: 20 -> 20, of which waited for: 9 -> 7; matrix products, arithmetic and copies ran while one was open for 7% -> 8% of each run, Pallas kernels for 21% -> 27%
where the time goes in v2:
time: 177 us; the launch traced here: 175 us
  Pallas kernels  50.2 us (28%)
  starting transfers between devices  35.4 us (20%)
  blocking collectives  29.7 us (17%)
  waiting for transfers between devices  27.9 us (16%)
  between operations  14.4 us (8%)
  other arithmetic  11.3 us (6%)
  local copies, waits for them, and re-layouts  4.9 us (3%)
    pallas_call x10, Pallas kernels, call(): pl.pallas_call(kernel, in_specs=[pl.BlockSpec(memory_space=pltpu.SMEM)] +...  50.2 us
    all_to_all x2, blocking collectives, spread(): return lax.all_to_all(t, axes, 0, 0, tiled=True).reshape(n, -1, 8, 128)  29.7 us
    all_to_all x4, starting transfers between devices, spread(): return lax.all_to_all(t, axes, 0, 0, tiled=True).reshape(n, -1, 8, 128)  22.1 us
    all_to_all x4, waiting for transfers between devices, spread(): return lax.all_to_all(t, axes, 0, 0, tiled=True).reshape(n, -1, 8, 128)  16 us
    ppermute x6, starting transfers between devices, body(): lax.ppermute(m, 'x', p)  10 us
    ppermute x1, waiting for transfers between devices, body(): got_b = lax.ppermute(sent_b, 'yl', SWAP)  6.13 us
    another operation x3, other arithmetic, body(): chol = jnp.linalg.cholesky(gram)  3.58 us
  transfers between devices with their start and end apart: 20, of which 7 were waited for; matrix products, arithmetic and copies ran while one was open for 8% of the time, Pallas kernels for 27%

profile of v2, /device:TPU:2, one launch (start us, length us, event | category | flops | bytes accessed | tf_op | source)
XLA Modules:
  0.0 174.7 jit_solution(2868336595236033054)
XLA Ops:
  7.2 0.0 all-gather.3.cloned.1.call-start
  7.2 0.7 all-gather.3.cloned.1.call-update
  7.9 0.6 pad_add_fusion.at
  8.5 4.9 %left_part.1 = (f32[32,8,128]{2,1,0:T(8,128)}, f32[32,8,128]{2,1,0:T(8,128)}) custom-call(s32[3]{0:T(128)} %pad_add_fusion.at, f32[32,4096]{1,0:T(8,128)} %bitcast.39, bf16[256,4096]{1,0:T(8,128)(2,1)} %cot.5, bf16[256,4096]{1,0:T(8,128)(2,1)} %bitcast.29, bf16[256,2048]{1,0:T(8,128)(2,1)} %ctx.4), custom_call_target="tpu_custom_call" | custom-call | flops 1 | bytes 1 | tf_op jit(solution)/shard_map/left_part/pallas_call | solution.py:108
  13.4 0.1 collective-permute-start
  13.5 3.0 %quarters.1 = (bf16[512,256]{1,0:T(8,128)(2,1)}, bf16[512,256]{1,0:T(8,128)(2,1)}, bf16[512,256]{1,0:T(8,128)(2,1)}, bf16[512,256]{1,0:T(8,128)(2,1)}) custom-call(s32[3]{0:T(128)} %pad_add_fusion.at, bf16[256,2048]{1,0:T(8,128)(2,1)} %ctx.4), custom_call_target="tpu_custom_call" | custom-call | flops 1 | bytes 1 | tf_op jit(solution)/shard_map/quarters/pallas_call | solution.py:108
  16.5 1.6 collective-permute-start.1
  18.0 0.9 collective-permute-start.2
  18.9 2.0 %collective-permute-start.3 = (bf16[512,256]{1,0:T(8,128)(2,1)}, bf16[512,256]{1,0:T(8,128)(2,1)S(1)}, u32[]{:S(2)}, u32[]{:S(2)}) collective-permute-start(bf16[512,256]{1,0:T(8,128)(2,1)} %get-tuple-element.80), channel_id=1, source_target_pairs={{0,4},{2,6},{4,0},{6,2},{1,5},{3,7},{5,1},{7,3},{8,12},{10,14},{12... | collective-permute-start | bytes 786440 | tf_op jit(solution)/shard_map/ppermute | solution.py:481
  20.9 0.0 collective-permute-done
  20.9 1.6 add.17
  22.5 8.3 %all-to-all-start = ((f32[32,8,128]{2,1,0:T(8,128)}), f32[32,8,128]{2,1,0:T(8,128)S(1)}, u32[]{:S(2)}, u32[]{:S(2)}) async-start(f32[32,8,128]{2,1,0:T(8,128)} %add.17), calls=%async_computation | async-start | bytes 262144 | tf_op jit(solution)/shard_map/all_to_all | solution.py:457
  30.7 2.9 %pick_half.1 = bf16[128,4096]{1,0:T(8,128)(2,1)} custom-call(s32[3]{0:T(128)} %pad_add_fusion.at, bf16[256,4096]{1,0:T(8,128)(2,1)} %w_own), custom_call_target="tpu_custom_call" | custom-call | flops 1 | bytes 1 | tf_op jit(solution)/shard_map/pick_half/pallas_call | solution.py:108
  33.6 0.0 collective-permute-done.1.refs_1_
  33.6 0.0 collective-permute-done.2.refs_2_
  33.6 2.1 %collective-permute-done.3.refs_3_ = bf16[512,256]{1,0:T(8,128)(2,1)S(1)} collective-permute-done((bf16[512,256]{1,0:T(8,128)(2,1)}, bf16[512,256]{1,0:T(8,128)(2,1)S(1)}, u32[]{:S(2)}, u32[]{:S(2)}) %collective-permute-start.3) | collective-permute-done | bytes 262176 | tf_op jit(solution)/shard_map/ppermute | solution.py:481
  35.8 4.0 %all-to-all-done = f32[32,8,128]{2,1,0:T(8,128)S(1)} async-done(((f32[32,8,128]{2,1,0:T(8,128)}), f32[32,8,128]{2,1,0:T(8,128)S(1)}, u32[]{:S(2)}, u32[]{:S(2)}) %all-to-all-start) | async-done | bytes 131104 | tf_op jit(solution)/shard_map/all_to_all | solution.py:457
  39.9 15.7 %all_to_all.30 = f32[64,8,128]{2,1,0:T(8,128)S(1)} all-to-all(f32[64,8,128]{2,1,0:T(8,128)S(1)} %bitcast.37), channel_id=1, replica_groups=mesh['yh'=2,'z'=8,'c'=2,'x'=4,'yl'=2] {'yh','x','yl'}, dimensions={0} | all-to-all | bytes 524288 | tf_op jit(solution)/shard_map/all_to_all | solution.py:457
  55.6 14.0 %all_to_all.31.own = f32[32,8,128]{2,1,0:T(8,128)S(1)} all-to-all(f32[32,8,128]{2,1,0:T(8,128)S(1)} %bitcast.42), channel_id=1, replica_groups=mesh['yh'=2,'z'=8,'c'=2,'x'=4,'yl'=2] {'z'}, dimensions={0} | all-to-all | bytes 262144 | tf_op jit(solution)/shard_map/all_to_all | solution.py:457
  69.6 0.4 collective-permute-start.6
  70.0 0.0 collective-permute-start.4
  70.0 1.3 collective-permute-done.4.other
  71.3 0.7 copy-done.14
  72.0 5.3 %right_part.1 = (f32[64,8,128]{2,1,0:T(8,128)}, f32[64,8,128]{2,1,0:T(8,128)}, f32[32,32]{1,0:T(8,128)}, f32[32,256]{1,0:T(8,128)}) custom-call(s32[3]{0:T(128)} %pad_add_fusion.at, f32[32,8,128]{2,1,0:T(8,128)} %copy-done.9, f32[32,8,128]{2,1,0:T(8,128)} %copy-done.14, bf16[256,2048]{1,0:T(8,128)(2,1)} %ctx.4, bf16[256,4096]{1,0:T(8,128)(2,1)} %cot.5, ...), custom_call_target="tpu_custom_call" | custom-call | flops 1 | bytes 1 | tf_op jit(solution)/shard_map/right_part/pallas_call | solution.py:108
  77.4 0.8 copy.10
  78.2 0.1 collective-permute-start.5
  78.3 0.7 fusion.3
  79.0 2.9 %cholesky.17 = f32[32,32]{1,0:T(8,128)S(1)} custom-call(f32[32,32]{1,0:T(8,128)S(1)} %fusion.3), custom_call_target="Cholesky" | custom-call | tf_op jit(solution)/shard_map/jit(cholesky)/cholesky | solution.py:497
  82.0 0.0 collective-permute-done.5
  82.0 1.7 add.18
  83.7 3.4 %all-to-all-start.3 = ((f32[64,8,128]{2,1,0:T(8,128)}), f32[64,8,128]{2,1,0:T(8,128)S(1)}, u32[]{:S(2)}, u32[]{:S(2)}) async-start(f32[64,8,128]{2,1,0:T(8,128)} %add.18), calls=%async_computation.3 | async-start | bytes 524288 | tf_op jit(solution)/shard_map/all_to_all | solution.py:457
  87.1 0.6 compare_reduce_fusion
  87.7 0.7 fusion
  88.4 2.4 %custom-call.6 = f32[1,32,32]{1,2,0:T(8,128)S(1)} custom-call(f32[1,32,32]{2,1,0:T(8,128)S(1)} %fusion), custom_call_target="InvertDiagBlocksLowerTriangular" | custom-call | tf_op jit(solution)/shard_map/triangular_solve | solution.py:498
  90.8 0.8 fusion.1.inv
  91.7 8.0 %all-to-all-done.3 = f32[64,8,128]{2,1,0:T(8,128)S(1)} async-done(((f32[64,8,128]{2,1,0:T(8,128)}), f32[64,8,128]{2,1,0:T(8,128)S(1)}, u32[]{:S(2)}, u32[]{:S(2)}) %all-to-all-start.3) | async-done | bytes 262176 | tf_op jit(solution)/shard_map/all_to_all | solution.py:457
  99.7 0.0 collective-permute-done.6.w_half
  99.7 0.1 collective-permute-start.7
  99.8 1.0 broadcast_in_dim.14
  100.8 6.8 %all-to-all-start.4 = ((f32[128,8,128]{2,1,0:T(8,128)}), f32[128,8,128]{2,1,0:T(8,128)S(1)}, u32[]{:S(2)}, u32[]{:S(2)}) async-start(f32[128,8,128]{2,1,0:T(8,128)} %bitcast.13), calls=%async_computation.4 | async-start | bytes 1048576 | tf_op jit(solution)/shard_map/all_to_all | solution.py:457
  107.6 0.0 all-gather.3.cloned.1.call-done
  107.6 5.5 %grad_chunk.3 = (bf16[256,1536]{1,0:T(8,128)(2,1)}, bf16[256,1536]{1,0:T(8,128)(2,1)}) custom-call(s32[3]{0:T(128)} %pad_add_fusion.at, bf16[512,256]{1,0:T(8,128)(2,1)} %get-tuple-element.98.refs_0_, bf16[512,256]{1,0:T(8,128)(2,1)} %copy-done, bf16[512,256]{1,0:T(8,128)(2,1)} %copy-done.1, bf16[512,256]{1,0:T(8,128)(2,1)} %copy-done.2, ...), custom_call_target="tpu_custom_call" | custom-call | flops 1610612736 | bytes 6291456 | tf_op jit(solution)/shard_map/grad_chunk/pallas_call | solution.py:108
  113.1 3.9 %all-to-all-done.4 = f32[128,8,128]{2,1,0:T(8,128)S(1)} async-done(((f32[128,8,128]{2,1,0:T(8,128)}), f32[128,8,128]{2,1,0:T(8,128)S(1)}, u32[]{:S(2)}, u32[]{:S(2)}) %all-to-all-start.4) | async-done | bytes 524320 | tf_op jit(solution)/shard_map/all_to_all | solution.py:457
  117.0 0.0 collective-permute-done.7.w_other
  117.0 0.3 collective-permute-start.9
  117.3 0.7 broadcast_in_dim.15
  118.1 3.6 %all-to-all-start.5 = ((f32[64,8,128]{2,1,0:T(8,128)}), f32[64,8,128]{2,1,0:T(8,128)S(1)}, u32[]{:S(2)}, u32[]{:S(2)}) async-start(f32[64,8,128]{2,1,0:T(8,128)} %bitcast.16), calls=%async_computation.5 | async-start | bytes 524288 | tf_op jit(solution)/shard_map/all_to_all | solution.py:457
  121.7 5.5 %grad_chunk.4 = (bf16[256,1536]{1,0:T(8,128)(2,1)}, bf16[256,1536]{1,0:T(8,128)(2,1)}) custom-call(s32[3]{0:T(128)} %pad_add_fusion.at, bf16[512,256]{1,0:T(8,128)(2,1)} %get-tuple-element.98.refs_0_, bf16[512,256]{1,0:T(8,128)(2,1)} %copy-done, bf16[512,256]{1,0:T(8,128)(2,1)} %copy-done.1, bf16[512,256]{1,0:T(8,128)(2,1)} %copy-done.2, ...), custom_call_target="tpu_custom_call" | custom-call | flops 1610612736 | bytes 6291456 | tf_op jit(solution)/shard_map/grad_chunk/pallas_call | solution.py:108
  127.2 1.8 %collective-permute-start.10 = (bf16[256,1536]{1,0:T(8,128)(2,1)}, bf16[256,1536]{1,0:T(8,128)(2,1)S(1)}, u32[]{:S(2)}, u32[]{:S(2)}) collective-permute-start(bf16[256,1536]{1,0:T(8,128)(2,1)} %get-tuple-element.120), channel_id=1, source_target_pairs={{0,1},{1,0},{2,3},{3,2},{4,5},{5,4},{6,7},{7,6},{8,9},{9,8},{10,11... | collective-permute-start | bytes 2359304 | tf_op jit(solution)/shard_map/ppermute | solution.py:514
  129.0 4.7 %grad_chunk.5 = (bf16[256,1024]{1,0:T(8,128)(2,1)}, bf16[256,1024]{1,0:T(8,128)(2,1)}) custom-call(s32[3]{0:T(128)} %pad_add_fusion.at, bf16[512,256]{1,0:T(8,128)(2,1)} %get-tuple-element.98.refs_0_, bf16[512,256]{1,0:T(8,128)(2,1)} %copy-done, bf16[512,256]{1,0:T(8,128)(2,1)} %copy-done.1, bf16[512,256]{1,0:T(8,128)(2,1)} %copy-done.2, ...), custom_call_target="tpu_custom_call" | custom-call | flops 1073741824 | bytes 4194304 | tf_op jit(solution)/shard_map/grad_chunk/pallas_call | solution.py:108
  133.8 0.0 all-to-all-done.5.own
  133.8 0.1 collective-permute-start.8
  133.9 0.4 collective-permute-start.11
  134.3 8.6 %ctx_blocks.1 = (bf16[256,512]{1,0:T(8,128)(2,1)}, bf16[256,512]{1,0:T(8,128)(2,1)}, bf16[256,512]{1,0:T(8,128)(2,1)}, bf16[256,512]{1,0:T(8,128)(2,1)}) custom-call(s32[3]{0:T(128)} %pad_add_fusion.at, bf16[256,4096]{1,0:T(8,128)(2,1)} %cot.5, bf16[256,4096]{1,0:T(8,128)(2,1)} %w_own, bf16[128,4096]{1,0:T(8,128)(2,1)} %copy-done.3, ...), custom_call_target="tpu_custom_call" | custom-call | flops 1 | bytes 1 | tf_op jit(solution)/shard_map/ctx_blocks/pallas_call | solution.py:108
  142.8 3.0 %collective-permute-start.12 = (bf16[256,512]{1,0:T(8,128)(2,1)}, bf16[256,512]{1,0:T(8,128)(2,1)S(1)}, u32[]{:S(2)}, u32[]{:S(2)}) collective-permute-start(bf16[256,512]{1,0:T(8,128)(2,1)} %get-tuple-element.124), channel_id=1, source_target_pairs={{2,0},{4,2},{6,4},{0,6},{3,1},{5,3},{7,5},{1,7},{10,8},{12,10},{14... | collective-permute-start | bytes 786440 | tf_op jit(solution)/shard_map/ppermute | solution.py:523
  145.9 2.6 %collective-permute-start.14 = (bf16[256,512]{1,0:T(8,128)(2,1)}, bf16[256,512]{1,0:T(8,128)(2,1)S(1)}, u32[]{:S(2)}, u32[]{:S(2)}) collective-permute-start(bf16[256,512]{1,0:T(8,128)(2,1)} %get-tuple-element.126), channel_id=1, source_target_pairs={{0,4},{2,6},{4,0},{6,2},{1,5},{3,7},{5,1},{7,3},{8,12},{10,14},{12... | collective-permute-start | bytes 786440 | tf_op jit(solution)/shard_map/ppermute | solution.py:523
  148.4 6.1 %collective-permute-done.10.refs_3_ = bf16[256,1536]{1,0:T(8,128)(2,1)S(1)} collective-permute-done((bf16[256,1536]{1,0:T(8,128)(2,1)}, bf16[256,1536]{1,0:T(8,128)(2,1)S(1)}, u32[]{:S(2)}, u32[]{:S(2)}) %collective-permute-start.10) | collective-permute-done | bytes 786464 | tf_op jit(solution)/shard_map/ppermute | solution.py:514
  154.6 0.9 copy-done.7
  155.5 6.1 %final_part.1 = (f32[32,4096]{1,0:T(8,128)}, bf16[192,256]{1,0:T(8,128)(2,1)}, bf16[256,4096]{1,0:T(8,128)(2,1)}, bf16[256,4096]{1,0:T(8,128)(2,1)}) custom-call(s32[3]{0:T(128)} %pad_add_fusion.at, f32[32,32]{1,0:T(8,128)} %fusion.1.inv, f32[32,256]{1,0:T(8,128)} %get-tuple-element.95.rows, f32[64,8,128]{2,1,0:T(8,128)} %copy-done.5, ...), custom_call_target="tpu_custom_call" | custom-call | flops 1 | bytes 1 | tf_op jit(solution)/shard_map/final_part/pallas_call | solution.py:108
  161.6 0.0 collective-permute-done.13.refs_1_
  161.6 0.0 collective-permute-done.14.refs_3_
  161.6 1.6 collective-permute-done.11.got
  163.3 0.8 copy-done.8
  164.1 3.7 %last_part.1 = (bf16[256,4096]{1,0:T(8,128)(2,1)}, bf16[256,2048]{1,0:T(8,128)(2,1)}) custom-call(s32[3]{0:T(128)} %pad_add_fusion.at, f32[32,4096]{1,0:T(8,128)} %get-tuple-element.128.basis, bf16[192,256]{1,0:T(8,128)(2,1)} %get-tuple-element.129.pb, bf16[256,1024]{1,0:T(8,128)(2,1)} %get-tuple-element.130.kept, ...), custom_call_target="tpu_custom_call", output_to_operand_aliasing={{0}: (9, {})} | custom-call | flops 1 | bytes 1 | tf_op jit(solution)/shard_map/last_part/pallas_call | solution.py:108
  (38 shorter events, 0.2 us)
Async XLA Ops:
  7.2 100.4 %all-gather.3.cloned.1.call-start = ((), (), s32[]{:S(2)}) async-start(), calls=%async_computation.6 | async-start | bytes 10485760 | tf_op jit(solution)/shard_map/all_gather | solution.py:474
  13.4 7.5 %collective-permute-start = (f32[32,8,128]{2,1,0:T(8,128)}, f32[32,8,128]{2,1,0:T(8,128)S(1)}, u32[]{:S(2)}, u32[]{:S(2)}) collective-permute-start(f32[32,8,128]{2,1,0:T(8,128)} %get-tuple-element.75), channel_id=1, source_target_pairs={{0,8},{8,0},{1,9},{9,1},{2,10},{10,2},{3,11},{11,3},{4,12},{12,4},... | collective-permute-start | bytes 393224 | tf_op jit(solution)/shard_map/ppermute | solution.py:482
  16.5 17.1 %collective-permute-start.1 = (bf16[512,256]{1,0:T(8,128)(2,1)}, bf16[512,256]{1,0:T(8,128)(2,1)S(1)}, u32[]{:S(2)}, u32[]{:S(2)}) collective-permute-start(bf16[512,256]{1,0:T(8,128)(2,1)} %get-tuple-element.78), channel_id=1, source_target_pairs={{0,2},{2,4},{4,6},{6,0},{1,3},{3,5},{5,7},{7,1},{8,10},{10,12},{12... | collective-permute-start | bytes 786440 | tf_op jit(solution)/shard_map/ppermute | solution.py:481
  18.0 15.6 %collective-permute-start.2 = (bf16[512,256]{1,0:T(8,128)(2,1)}, bf16[512,256]{1,0:T(8,128)(2,1)S(1)}, u32[]{:S(2)}, u32[]{:S(2)}) collective-permute-start(bf16[512,256]{1,0:T(8,128)(2,1)} %get-tuple-element.79), channel_id=1, source_target_pairs={{2,0},{4,2},{6,4},{0,6},{3,1},{5,3},{7,5},{1,7},{10,8},{12,10},{14... | collective-permute-start | bytes 786440 | tf_op jit(solution)/shard_map/ppermute | solution.py:481
  18.9 16.9 %collective-permute-start.3 = (bf16[512,256]{1,0:T(8,128)(2,1)}, bf16[512,256]{1,0:T(8,128)(2,1)S(1)}, u32[]{:S(2)}, u32[]{:S(2)}) collective-permute-start(bf16[512,256]{1,0:T(8,128)(2,1)} %get-tuple-element.80), channel_id=1, source_target_pairs={{0,4},{2,6},{4,0},{6,2},{1,5},{3,7},{5,1},{7,3},{8,12},{10,14},{12... | collective-permute-start | bytes 786440 | tf_op jit(solution)/shard_map/ppermute | solution.py:481
  22.5 17.4 %all-to-all-start = ((f32[32,8,128]{2,1,0:T(8,128)}), f32[32,8,128]{2,1,0:T(8,128)S(1)}, u32[]{:S(2)}, u32[]{:S(2)}) async-start(f32[32,8,128]{2,1,0:T(8,128)} %add.17), calls=%async_computation | async-start | bytes 262144 | tf_op jit(solution)/shard_map/all_to_all | solution.py:457
  33.6 43.7 %copy-start = (bf16[512,256]{1,0:T(8,128)(2,1)}, bf16[512,256]{1,0:T(8,128)(2,1)S(1)}, u32[]{:S(2)}) copy-start(bf16[512,256]{1,0:T(8,128)(2,1)S(1)} %collective-permute-done.1.refs_1_) | copy-start | bytes 786436
  33.6 43.7 %copy-start.1 = (bf16[512,256]{1,0:T(8,128)(2,1)}, bf16[512,256]{1,0:T(8,128)(2,1)S(1)}, u32[]{:S(2)}) copy-start(bf16[512,256]{1,0:T(8,128)(2,1)S(1)} %collective-permute-done.2.refs_2_) | copy-start | bytes 786436
  35.8 41.6 %copy-start.2 = (bf16[512,256]{1,0:T(8,128)(2,1)}, bf16[512,256]{1,0:T(8,128)(2,1)S(1)}, u32[]{:S(2)}) copy-start(bf16[512,256]{1,0:T(8,128)(2,1)S(1)} %collective-permute-done.3.refs_3_) | copy-start | bytes 786436
  69.6 1.7 copy-start.9
  69.6 30.1 %collective-permute-start.6 = (bf16[128,4096]{1,0:T(8,128)(2,1)}, bf16[128,4096]{1,0:T(8,128)(2,1)S(1)}, u32[]{:S(2)}, u32[]{:S(2)}) collective-permute-start(bf16[128,4096]{1,0:T(8,128)(2,1)} %pick_half.1), channel_id=1, source_target_pairs={{0,1},{1,0},{2,3},{3,2},{4,5},{5,4},{6,7},{7,6},{8,9},{9,8},{10,11... | collective-permute-start | bytes 3145736 | tf_op jit(solution)/shard_map/ppermute | solution.py:491
  70.0 1.3 collective-permute-start.4
  71.3 0.7 copy-start.14
  78.2 3.8 %collective-permute-start.5 = (f32[64,8,128]{2,1,0:T(8,128)}, f32[64,8,128]{2,1,0:T(8,128)S(1)}, u32[]{:S(2)}, u32[]{:S(2)}) collective-permute-start(f32[64,8,128]{2,1,0:T(8,128)} %get-tuple-element.91), channel_id=1, source_target_pairs={{0,8},{8,0},{1,9},{9,1},{2,10},{10,2},{3,11},{11,3},{4,12},{12,4},... | collective-permute-start | bytes 786440 | tf_op jit(solution)/shard_map/ppermute | solution.py:496
  83.7 16.0 %all-to-all-start.3 = ((f32[64,8,128]{2,1,0:T(8,128)}), f32[64,8,128]{2,1,0:T(8,128)S(1)}, u32[]{:S(2)}, u32[]{:S(2)}) async-start(f32[64,8,128]{2,1,0:T(8,128)} %add.18), calls=%async_computation.3 | async-start | bytes 524288 | tf_op jit(solution)/shard_map/all_to_all | solution.py:457
  99.7 13.4 %copy-start.3 = (bf16[128,4096]{1,0:T(8,128)(2,1)}, bf16[128,4096]{1,0:T(8,128)(2,1)S(1)}, u32[]{:S(2)}) copy-start(bf16[128,4096]{1,0:T(8,128)(2,1)S(1)} %collective-permute-done.6.w_half) | copy-start | bytes 3145732
  99.7 17.3 %collective-permute-start.7 = (bf16[128,4096]{1,0:T(8,128)(2,1)S(1)}, bf16[128,4096]{1,0:T(8,128)(2,1)S(1)}, u32[]{:S(2)}, u32[]{:S(2)}) collective-permute-start(bf16[128,4096]{1,0:T(8,128)(2,1)S(1)} %collective-permute-done.6.w_half), channel_id=1, source_target_pairs={{0,8},{8,0},{1,9},{9,1},{2,10},{10,2},{3,11},{11,3},{4,12},{12,4},... | collective-permute-start | bytes 3145736 | tf_op jit(solution)/shard_map/ppermute | solution.py:503
  100.8 16.3 %all-to-all-start.4 = ((f32[128,8,128]{2,1,0:T(8,128)}), f32[128,8,128]{2,1,0:T(8,128)S(1)}, u32[]{:S(2)}, u32[]{:S(2)}) async-start(f32[128,8,128]{2,1,0:T(8,128)} %bitcast.13), calls=%async_computation.4 | async-start | bytes 1048576 | tf_op jit(solution)/shard_map/all_to_all | solution.py:457
  117.0 10.2 %copy-start.4 = (bf16[128,4096]{1,0:T(8,128)(2,1)}, bf16[128,4096]{1,0:T(8,128)(2,1)S(1)}, u32[]{:S(2)}) copy-start(bf16[128,4096]{1,0:T(8,128)(2,1)S(1)} %collective-permute-done.7.w_other) | copy-start | bytes 3145732
  117.0 28.8 %collective-permute-start.9 = (bf16[256,1536]{1,0:T(8,128)(2,1)}, bf16[256,1536]{1,0:T(8,128)(2,1)S(1)}, u32[]{:S(2)}, u32[]{:S(2)}) collective-permute-start(bf16[256,1536]{1,0:T(8,128)(2,1)} %get-tuple-element.119), channel_id=1, source_target_pairs={{0,1},{1,0},{2,3},{3,2},{4,5},{5,4},{6,7},{7,6},{8,9},{9,8},{10,11... | collective-permute-start | bytes 2359304 | tf_op jit(solution)/shard_map/ppermute | solution.py:509
  118.1 15.7 %all-to-all-start.5 = ((f32[64,8,128]{2,1,0:T(8,128)}), f32[64,8,128]{2,1,0:T(8,128)S(1)}, u32[]{:S(2)}, u32[]{:S(2)}) async-start(f32[64,8,128]{2,1,0:T(8,128)} %bitcast.16), calls=%async_computation.5 | async-start | bytes 524288 | tf_op jit(solution)/shard_map/all_to_all | solution.py:457
  127.2 27.4 %collective-permute-start.10 = (bf16[256,1536]{1,0:T(8,128)(2,1)}, bf16[256,1536]{1,0:T(8,128)(2,1)S(1)}, u32[]{:S(2)}, u32[]{:S(2)}) collective-permute-start(bf16[256,1536]{1,0:T(8,128)(2,1)} %get-tuple-element.120), channel_id=1, source_target_pairs={{0,1},{1,0},{2,3},{3,2},{4,5},{5,4},{6,7},{7,6},{8,9},{9,8},{10,11... | collective-permute-start | bytes 2359304 | tf_op jit(solution)/shard_map/ppermute | solution.py:514
  133.8 9.1 %copy-start.5 = (f32[64,8,128]{2,1,0:T(8,128)}, f32[64,8,128]{2,1,0:T(8,128)S(1)}, u32[]{:S(2)}) copy-start(f32[64,8,128]{2,1,0:T(8,128)S(1)} %all-to-all-done.5.own) | copy-start | bytes 786436
  133.8 9.1 %collective-permute-start.8 = (f32[64,8,128]{2,1,0:T(8,128)S(1)}, f32[64,8,128]{2,1,0:T(8,128)S(1)}, u32[]{:S(2)}, u32[]{:S(2)}) collective-permute-start(f32[64,8,128]{2,1,0:T(8,128)S(1)} %all-to-all-done.5.own), channel_id=1, source_target_pairs={{0,8},{8,0},{1,9},{9,1},{2,10},{10,2},{3,11},{11,3},{4,12},{12,4},... | collective-permute-start | bytes 786440 | tf_op jit(solution)/shard_map/ppermute | solution.py:519
  133.9 29.4 %collective-permute-start.11 = (bf16[256,1024]{1,0:T(8,128)(2,1)}, bf16[256,1024]{1,0:T(8,128)(2,1)S(1)}, u32[]{:S(2)}, u32[]{:S(2)}) collective-permute-start(bf16[256,1024]{1,0:T(8,128)(2,1)} %get-tuple-element.122), channel_id=1, source_target_pairs={{0,1},{1,0},{2,3},{3,2},{4,5},{5,4},{6,7},{7,6},{8,9},{9,8},{10,11... | collective-permute-start | bytes 1572872 | tf_op jit(solution)/shard_map/ppermute | solution.py:518
  142.8 11.7 %copy-start.12 = (f32[64,8,128]{2,1,0:T(8,128)}, f32[64,8,128]{2,1,0:T(8,128)S(1)}, u32[]{:S(2)}) copy-start(f32[64,8,128]{2,1,0:T(8,128)S(1)} %collective-permute-done.8.other) | copy-start | bytes 786436
  142.8 18.7 %collective-permute-start.12 = (bf16[256,512]{1,0:T(8,128)(2,1)}, bf16[256,512]{1,0:T(8,128)(2,1)S(1)}, u32[]{:S(2)}, u32[]{:S(2)}) collective-permute-start(bf16[256,512]{1,0:T(8,128)(2,1)} %get-tuple-element.124), channel_id=1, source_target_pairs={{2,0},{4,2},{6,4},{0,6},{3,1},{5,3},{7,5},{1,7},{10,8},{12,10},{14... | collective-permute-start | bytes 786440 | tf_op jit(solution)/shard_map/ppermute | solution.py:523
  145.8 15.7 %collective-permute-start.13 = (bf16[256,512]{1,0:T(8,128)(2,1)}, bf16[256,512]{1,0:T(8,128)(2,1)S(1)}, u32[]{:S(2)}, u32[]{:S(2)}) collective-permute-start(bf16[256,512]{1,0:T(8,128)(2,1)} %get-tuple-element.125), channel_id=1, source_target_pairs={{0,2},{2,4},{4,6},{6,0},{1,3},{3,5},{5,7},{7,1},{8,10},{10,12},{12... | collective-permute-start | bytes 786440 | tf_op jit(solution)/shard_map/ppermute | solution.py:523
  145.9 8.7 %copy-start.6 = (bf16[256,1536]{1,0:T(8,128)(2,1)}, bf16[256,1536]{1,0:T(8,128)(2,1)S(1)}, u32[]{:S(2)}) copy-start(bf16[256,1536]{1,0:T(8,128)(2,1)S(1)} %collective-permute-done.9.refs_2_) | copy-start | bytes 2359300
  145.9 15.7 %collective-permute-start.14 = (bf16[256,512]{1,0:T(8,128)(2,1)}, bf16[256,512]{1,0:T(8,128)(2,1)S(1)}, u32[]{:S(2)}, u32[]{:S(2)}) collective-permute-start(bf16[256,512]{1,0:T(8,128)(2,1)} %get-tuple-element.126), channel_id=1, source_target_pairs={{0,4},{2,6},{4,0},{6,2},{1,5},{3,7},{5,1},{7,3},{8,12},{10,14},{12... | collective-permute-start | bytes 786440 | tf_op jit(solution)/shard_map/ppermute | solution.py:523
  154.6 0.9 copy-start.7
  161.6 1.7 copy-start.10
  161.6 1.7 copy-start.11
  161.6 1.6 copy-start.13
  163.2 0.8 copy-start.8
Sparse Core Ops, SparseCore 0:
  9.8 94.1 all-gather.2

commit v3 on v2

--- a/solution.py
+++ b/solution.py
@@ -103,7 +103,7 @@
         copy.wait()
 
 
-def call(kernel, name, ins, outs, scratch, flops, size, alias=None, hide=False):
+def call(kernel, name, ins, outs, scratch, flops, size, alias=None, hide=False, vmem=VMEM):
     spec = lambda inside: pl.BlockSpec(memory_space=pltpu.VMEM if inside else pl.ANY)
     return pl.pallas_call(
         kernel,
@@ -112,7 +112,7 @@
         out_shape=[jax.ShapeDtypeStruct(shape, dtype) for shape, dtype, _ in outs],
         scratch_shapes=scratch,
         input_output_aliases=alias or {},
-        compiler_params=params(),
+        compiler_params=params(vmem),
         cost_estimate=cost(flops, size) if hide else cost(1, 1),
         name=name,
     )(*[a for a, _ in ins])
@@ -449,6 +449,7 @@
         2 * 256 * 256 * 1024,
         4 << 20,
         {9: 0},
+        vmem=8 << 20,
     )
 
 
@@ -504,7 +505,7 @@
     got = collect(jnp.sum(got, 0), ("yh", "x", "yl"))
     grad = lambda i: grad_chunk(at, ctx_x, cotangent, error, wide, STARTS[i], SPLIT[i])
     kept_a, sent_a = grad(0)
-    got, other, kept_a, sent_a = fence((got, other, kept_a, sent_a))
+    got, other, kept_a = fence((got, other, kept_a))
 
     got_a = lax.ppermute(sent_a, "yl", SWAP)
     out, late = fence((copies_for(jnp.sum(got, 0), "z"), wide))
@@ -518,7 +519,7 @@
     got_c = lax.ppermute(sent_c, "yl", SWAP)
     qo = lax.ppermute(qt, "c", SWAP)
     blocks = ctx_blocks(at, cotangent, wide, [weight, half, other])
-    qo, blocks = fence((qo, blocks))
+    qo, blocks, got_a = fence((qo, blocks, got_a))
     back = (LEFT, RIGHT, OPPOSITE)
     home = [blocks[0]] + [lax.ppermute(m, "x", p) for m, p in zip(blocks[1:], back)]
     new_basis, pb, update, partial = final_part(

time: 177 us -> 176 us (level)
  waiting for transfers between devices: 27.9 us -> 24.7 us
    ppermute x1, waiting for transfers between devices: 6.13 us -> 2.43 us  [body(): got_b = lax.ppermute(sent_b, 'yl', SWAP)]
    ppermute x1, waiting for transfers between devices: 1.63 us -> 3.67 us  [body(): got_c = lax.ppermute(sent_c, 'yl', SWAP)]
  transfers between devices with their start and end apart: 20 -> 20, of which waited for: 7 -> 7; matrix products, arithmetic and copies ran while one was open for 8% -> 9% of each run, Pallas kernels for 27% -> 27%
where the time goes in v3:
time: 176 us; the launch traced here: 173 us
  Pallas kernels  48.9 us (28%)
  starting transfers between devices  36.7 us (21%)
  blocking collectives  29.8 us (17%)
  waiting for transfers between devices  24.7 us (14%)
  between operations  14.4 us (8%)
  other arithmetic  11.4 us (6%)
  local copies, waits for them, and re-layouts  6.08 us (3%)
    pallas_call x10, Pallas kernels, call(): pl.pallas_call(kernel, in_specs=[pl.BlockSpec(memory_space=pltpu.SMEM)] +...  48.9 us
    all_to_all x2, blocking collectives, spread(): return lax.all_to_all(t, axes, 0, 0, tiled=True).reshape(n, -1, 8, 128)  29.8 us
    all_to_all x4, starting transfers between devices, spread(): return lax.all_to_all(t, axes, 0, 0, tiled=True).reshape(n, -1, 8, 128)  22.1 us
    all_to_all x4, waiting for transfers between devices, spread(): return lax.all_to_all(t, axes, 0, 0, tiled=True).reshape(n, -1, 8, 128)  14.3 us
    ppermute x6, starting transfers between devices, body(): lax.ppermute(m, 'x', p)  10 us
    ppermute x1, waiting for transfers between devices, body(): got_c = lax.ppermute(sent_c, 'yl', SWAP)  3.67 us
    another operation x3, other arithmetic, body(): chol = jnp.linalg.cholesky(gram)  3.58 us
  transfers between devices with their start and end apart: 20, of which 7 were waited for; matrix products, arithmetic and copies ran while one was open for 9% of the time, Pallas kernels for 27%

profile of v3, /device:TPU:2, one launch (start us, length us, event | category | flops | bytes accessed | tf_op | source)
XLA Modules:
  0.0 172.9 jit_solution(15879619331830311347)
XLA Ops:
  7.2 0.0 all-gather.3.cloned.1.call-start
  7.2 0.7 all-gather.3.cloned.1.call-update
  7.9 0.6 pad_add_fusion.at
  8.6 4.9 %left_part.1 = (f32[32,8,128]{2,1,0:T(8,128)}, f32[32,8,128]{2,1,0:T(8,128)}) custom-call(s32[3]{0:T(128)} %pad_add_fusion.at, f32[32,4096]{1,0:T(8,128)} %bitcast.40, bf16[256,4096]{1,0:T(8,128)(2,1)} %cot.5, bf16[256,4096]{1,0:T(8,128)(2,1)} %bitcast.30, bf16[256,2048]{1,0:T(8,128)(2,1)} %ctx.4), custom_call_target="tpu_custom_call" | custom-call | flops 1 | bytes 1 | tf_op jit(solution)/shard_map/left_part/pallas_call | solution.py:108
  13.5 0.1 collective-permute-start
  13.6 3.0 %quarters.1 = (bf16[512,256]{1,0:T(8,128)(2,1)}, bf16[512,256]{1,0:T(8,128)(2,1)}, bf16[512,256]{1,0:T(8,128)(2,1)}, bf16[512,256]{1,0:T(8,128)(2,1)}) custom-call(s32[3]{0:T(128)} %pad_add_fusion.at, bf16[256,2048]{1,0:T(8,128)(2,1)} %ctx.4), custom_call_target="tpu_custom_call" | custom-call | flops 1 | bytes 1 | tf_op jit(solution)/shard_map/quarters/pallas_call | solution.py:108
  16.6 1.6 collective-permute-start.1
  18.1 0.9 collective-permute-start.2
  19.0 2.0 %collective-permute-start.3 = (bf16[512,256]{1,0:T(8,128)(2,1)}, bf16[512,256]{1,0:T(8,128)(2,1)S(1)}, u32[]{:S(2)}, u32[]{:S(2)}) collective-permute-start(bf16[512,256]{1,0:T(8,128)(2,1)} %get-tuple-element.80), channel_id=1, source_target_pairs={{0,4},{2,6},{4,0},{6,2},{1,5},{3,7},{5,1},{7,3},{8,12},{10,14},{12... | collective-permute-start | bytes 786440 | tf_op jit(solution)/shard_map/ppermute | solution.py:482
  21.0 0.0 collective-permute-done
  21.0 1.6 add.17
  22.6 8.3 %all-to-all-start = ((f32[32,8,128]{2,1,0:T(8,128)}), f32[32,8,128]{2,1,0:T(8,128)S(1)}, u32[]{:S(2)}, u32[]{:S(2)}) async-start(f32[32,8,128]{2,1,0:T(8,128)} %add.17), calls=%async_computation | async-start | bytes 262144 | tf_op jit(solution)/shard_map/all_to_all | solution.py:458
  30.8 2.9 %pick_half.1 = bf16[128,4096]{1,0:T(8,128)(2,1)} custom-call(s32[3]{0:T(128)} %pad_add_fusion.at, bf16[256,4096]{1,0:T(8,128)(2,1)} %w_own), custom_call_target="tpu_custom_call" | custom-call | flops 1 | bytes 1 | tf_op jit(solution)/shard_map/pick_half/pallas_call | solution.py:108
  33.7 0.0 collective-permute-done.1.refs_1_
  33.7 0.0 collective-permute-done.2.refs_2_
  33.7 2.2 %collective-permute-done.3.refs_3_ = bf16[512,256]{1,0:T(8,128)(2,1)S(1)} collective-permute-done((bf16[512,256]{1,0:T(8,128)(2,1)}, bf16[512,256]{1,0:T(8,128)(2,1)S(1)}, u32[]{:S(2)}, u32[]{:S(2)}) %collective-permute-start.3) | collective-permute-done | bytes 262176 | tf_op jit(solution)/shard_map/ppermute | solution.py:482
  36.0 3.9 %all-to-all-done = f32[32,8,128]{2,1,0:T(8,128)S(1)} async-done(((f32[32,8,128]{2,1,0:T(8,128)}), f32[32,8,128]{2,1,0:T(8,128)S(1)}, u32[]{:S(2)}, u32[]{:S(2)}) %all-to-all-start) | async-done | bytes 131104 | tf_op jit(solution)/shard_map/all_to_all | solution.py:458
  39.9 15.7 %all_to_all.30 = f32[64,8,128]{2,1,0:T(8,128)S(1)} all-to-all(f32[64,8,128]{2,1,0:T(8,128)S(1)} %bitcast.38), channel_id=1, replica_groups=mesh['yh'=2,'z'=8,'c'=2,'x'=4,'yl'=2] {'yh','x','yl'}, dimensions={0} | all-to-all | bytes 524288 | tf_op jit(solution)/shard_map/all_to_all | solution.py:458
  55.7 14.0 %all_to_all.31.own = f32[32,8,128]{2,1,0:T(8,128)S(1)} all-to-all(f32[32,8,128]{2,1,0:T(8,128)S(1)} %bitcast.42), channel_id=1, replica_groups=mesh['yh'=2,'z'=8,'c'=2,'x'=4,'yl'=2] {'z'}, dimensions={0} | all-to-all | bytes 262144 | tf_op jit(solution)/shard_map/all_to_all | solution.py:458
  69.8 0.4 collective-permute-start.6
  70.2 0.0 collective-permute-start.4
  70.2 1.3 collective-permute-done.4.other
  71.5 0.7 copy-done.14
  72.2 5.3 %right_part.1 = (f32[64,8,128]{2,1,0:T(8,128)}, f32[64,8,128]{2,1,0:T(8,128)}, f32[32,32]{1,0:T(8,128)}, f32[32,256]{1,0:T(8,128)}) custom-call(s32[3]{0:T(128)} %pad_add_fusion.at, f32[32,8,128]{2,1,0:T(8,128)} %copy-done.12, f32[32,8,128]{2,1,0:T(8,128)} %copy-done.14, bf16[256,2048]{1,0:T(8,128)(2,1)} %ctx.4, bf16[256,4096]{1,0:T(8,128)(2,1)} %cot.5, ...), custom_call_target="tpu_custom_call" | custom-call | flops 1 | bytes 1 | tf_op jit(solution)/shard_map/right_part/pallas_call | solution.py:108
  77.5 0.8 copy.10
  78.3 0.1 collective-permute-start.5
  78.5 0.7 fusion.3
  79.2 2.9 %cholesky.17 = f32[32,32]{1,0:T(8,128)S(1)} custom-call(f32[32,32]{1,0:T(8,128)S(1)} %fusion.3), custom_call_target="Cholesky" | custom-call | tf_op jit(solution)/shard_map/jit(cholesky)/cholesky | solution.py:498
  82.2 1.7 add.18
  83.9 3.4 %all-to-all-start.3 = ((f32[64,8,128]{2,1,0:T(8,128)}), f32[64,8,128]{2,1,0:T(8,128)S(1)}, u32[]{:S(2)}, u32[]{:S(2)}) async-start(f32[64,8,128]{2,1,0:T(8,128)} %add.18), calls=%async_computation.3 | async-start | bytes 524288 | tf_op jit(solution)/shard_map/all_to_all | solution.py:458
  87.3 0.6 compare_reduce_fusion
  87.9 0.7 fusion
  88.6 2.4 %custom-call.6 = f32[1,32,32]{1,2,0:T(8,128)S(1)} custom-call(f32[1,32,32]{2,1,0:T(8,128)S(1)} %fusion), custom_call_target="InvertDiagBlocksLowerTriangular" | custom-call | tf_op jit(solution)/shard_map/triangular_solve | solution.py:499
  91.0 0.8 fusion.1.inv
  91.8 8.0 %all-to-all-done.3 = f32[64,8,128]{2,1,0:T(8,128)S(1)} async-done(((f32[64,8,128]{2,1,0:T(8,128)}), f32[64,8,128]{2,1,0:T(8,128)S(1)}, u32[]{:S(2)}, u32[]{:S(2)}) %all-to-all-start.3) | async-done | bytes 262176 | tf_op jit(solution)/shard_map/all_to_all | solution.py:458
  99.9 0.1 collective-permute-start.7
  100.0 1.0 broadcast_in_dim.14
  100.9 6.8 %all-to-all-start.4 = ((f32[128,8,128]{2,1,0:T(8,128)}), f32[128,8,128]{2,1,0:T(8,128)S(1)}, u32[]{:S(2)}, u32[]{:S(2)}) async-start(f32[128,8,128]{2,1,0:T(8,128)} %bitcast.13), calls=%async_computation.4 | async-start | bytes 1048576 | tf_op jit(solution)/shard_map/all_to_all | solution.py:458
  107.8 0.0 all-gather.3.cloned.1.call-done
  107.8 5.5 %grad_chunk.3 = (bf16[256,1536]{1,0:T(8,128)(2,1)}, bf16[256,1536]{1,0:T(8,128)(2,1)}) custom-call(s32[3]{0:T(128)} %pad_add_fusion.at, bf16[512,256]{1,0:T(8,128)(2,1)} %get-tuple-element.98.refs_0_, bf16[512,256]{1,0:T(8,128)(2,1)} %copy-done.5, bf16[512,256]{1,0:T(8,128)(2,1)} %copy-done.6, bf16[512,256]{1,0:T(8,128)(2,1)} %copy-done.7, ...), custom_call_target="tpu_custom_call" | custom-call | flops 1610612736 | bytes 6291456 | tf_op jit(solution)/shard_map/grad_chunk/pallas_call | solution.py:108
  113.3 1.5 collective-permute-start.9
  114.8 2.4 %all-to-all-done.4 = f32[128,8,128]{2,1,0:T(8,128)S(1)} async-done(((f32[128,8,128]{2,1,0:T(8,128)}), f32[128,8,128]{2,1,0:T(8,128)S(1)}, u32[]{:S(2)}, u32[]{:S(2)}) %all-to-all-start.4) | async-done | bytes 524320 | tf_op jit(solution)/shard_map/all_to_all | solution.py:458
  117.2 0.8 broadcast_in_dim.15
  118.0 3.6 %all-to-all-start.5 = ((f32[64,8,128]{2,1,0:T(8,128)}), f32[64,8,128]{2,1,0:T(8,128)S(1)}, u32[]{:S(2)}, u32[]{:S(2)}) async-start(f32[64,8,128]{2,1,0:T(8,128)} %bitcast.16), calls=%async_computation.5 | async-start | bytes 524288 | tf_op jit(solution)/shard_map/all_to_all | solution.py:458
  121.6 5.5 %grad_chunk.4 = (bf16[256,1536]{1,0:T(8,128)(2,1)}, bf16[256,1536]{1,0:T(8,128)(2,1)}) custom-call(s32[3]{0:T(128)} %pad_add_fusion.at, bf16[512,256]{1,0:T(8,128)(2,1)} %get-tuple-element.98.refs_0_, bf16[512,256]{1,0:T(8,128)(2,1)} %copy-done.5, bf16[512,256]{1,0:T(8,128)(2,1)} %copy-done.6, bf16[512,256]{1,0:T(8,128)(2,1)} %copy-done.7, ...), custom_call_target="tpu_custom_call" | custom-call | flops 1610612736 | bytes 6291456 | tf_op jit(solution)/shard_map/grad_chunk/pallas_call | solution.py:108
  127.2 0.4 collective-permute-start.10
  127.6 4.8 %grad_chunk.5 = (bf16[256,1024]{1,0:T(8,128)(2,1)}, bf16[256,1024]{1,0:T(8,128)(2,1)}) custom-call(s32[3]{0:T(128)} %pad_add_fusion.at, bf16[512,256]{1,0:T(8,128)(2,1)} %get-tuple-element.98.refs_0_, bf16[512,256]{1,0:T(8,128)(2,1)} %copy-done.5, bf16[512,256]{1,0:T(8,128)(2,1)} %copy-done.6, bf16[512,256]{1,0:T(8,128)(2,1)} %copy-done.7, ...), custom_call_target="tpu_custom_call" | custom-call | flops 1073741824 | bytes 4194304 | tf_op jit(solution)/shard_map/grad_chunk/pallas_call | solution.py:108
  132.3 0.0 all-to-all-done.5.own
  132.3 0.1 collective-permute-start.8
  132.4 1.8 %collective-permute-start.11 = (bf16[256,1024]{1,0:T(8,128)(2,1)}, bf16[256,1024]{1,0:T(8,128)(2,1)S(1)}, u32[]{:S(2)}, u32[]{:S(2)}) collective-permute-start(bf16[256,1024]{1,0:T(8,128)(2,1)} %get-tuple-element.122), channel_id=1, source_target_pairs={{0,1},{1,0},{2,3},{3,2},{4,5},{5,4},{6,7},{7,6},{8,9},{9,8},{10,11... | collective-permute-start | bytes 1572872 | tf_op jit(solution)/shard_map/ppermute | solution.py:519
  134.3 8.5 %ctx_blocks.1 = (bf16[256,512]{1,0:T(8,128)(2,1)}, bf16[256,512]{1,0:T(8,128)(2,1)}, bf16[256,512]{1,0:T(8,128)(2,1)}, bf16[256,512]{1,0:T(8,128)(2,1)}) custom-call(s32[3]{0:T(128)} %pad_add_fusion.at, bf16[256,4096]{1,0:T(8,128)(2,1)} %cot.5, bf16[256,4096]{1,0:T(8,128)(2,1)} %w_own, bf16[128,4096]{1,0:T(8,128)(2,1)} %copy-done.8, ...), custom_call_target="tpu_custom_call" | custom-call | flops 1 | bytes 1 | tf_op jit(solution)/shard_map/ctx_blocks/pallas_call | solution.py:108
  142.9 0.0 collective-permute-done.9.refs_2_
  142.9 2.8 %collective-permute-start.12 = (bf16[256,512]{1,0:T(8,128)(2,1)}, bf16[256,512]{1,0:T(8,128)(2,1)S(1)}, u32[]{:S(2)}, u32[]{:S(2)}) collective-permute-start(bf16[256,512]{1,0:T(8,128)(2,1)} %get-tuple-element.124), channel_id=1, source_target_pairs={{2,0},{4,2},{6,4},{0,6},{3,1},{5,3},{7,5},{1,7},{10,8},{12,10},{14... | collective-permute-start | bytes 786440 | tf_op jit(solution)/shard_map/ppermute | solution.py:524
  145.7 0.0 collective-permute-start.13
  145.7 2.8 %collective-permute-start.14 = (bf16[256,512]{1,0:T(8,128)(2,1)}, bf16[256,512]{1,0:T(8,128)(2,1)S(1)}, u32[]{:S(2)}, u32[]{:S(2)}) collective-permute-start(bf16[256,512]{1,0:T(8,128)(2,1)} %get-tuple-element.126), channel_id=1, source_target_pairs={{0,4},{2,6},{4,0},{6,2},{1,5},{3,7},{5,1},{7,3},{8,12},{10,14},{12... | collective-permute-start | bytes 786440 | tf_op jit(solution)/shard_map/ppermute | solution.py:524
  148.4 2.4 %collective-permute-done.10.refs_3_ = bf16[256,1536]{1,0:T(8,128)(2,1)S(1)} collective-permute-done((bf16[256,1536]{1,0:T(8,128)(2,1)}, bf16[256,1536]{1,0:T(8,128)(2,1)S(1)}, u32[]{:S(2)}, u32[]{:S(2)}) %collective-permute-start.10) | collective-permute-done | bytes 786464 | tf_op jit(solution)/shard_map/ppermute | solution.py:515
  150.9 0.9 copy-done.11
  151.8 6.1 %final_part.1 = (f32[32,4096]{1,0:T(8,128)}, bf16[192,256]{1,0:T(8,128)(2,1)}, bf16[256,4096]{1,0:T(8,128)(2,1)}, bf16[256,4096]{1,0:T(8,128)(2,1)}) custom-call(s32[3]{0:T(128)} %pad_add_fusion.at, f32[32,32]{1,0:T(8,128)} %fusion.1.inv, f32[32,256]{1,0:T(8,128)} %get-tuple-element.95.rows, f32[64,8,128]{2,1,0:T(8,128)} %copy-done.10, ...), custom_call_target="tpu_custom_call" | custom-call | flops 1 | bytes 1 | tf_op jit(solution)/shard_map/final_part/pallas_call | solution.py:108
  157.8 3.7 %collective-permute-done.11.got = bf16[256,1024]{1,0:T(8,128)(2,1)S(1)} collective-permute-done((bf16[256,1024]{1,0:T(8,128)(2,1)}, bf16[256,1024]{1,0:T(8,128)(2,1)S(1)}, u32[]{:S(2)}, u32[]{:S(2)}) %collective-permute-start.11) | collective-permute-done | bytes 524320 | tf_op jit(solution)/shard_map/ppermute | solution.py:519
  161.5 0.0 collective-permute-done.14.refs_3_
  161.5 0.0 copy-start.1
  161.6 1.0 copy-done.1
  162.6 0.9 copy-done.3
  163.5 2.5 %last_part.1 = (bf16[256,4096]{1,0:T(8,128)(2,1)}, bf16[256,2048]{1,0:T(8,128)(2,1)}) custom-call(s32[3]{0:T(128)S(1)} %copy-done.4, f32[32,4096]{1,0:T(8,128)S(1)} %copy-done.1, bf16[192,256]{1,0:T(8,128)(2,1)S(1)} %copy-done.3, bf16[256,1024]{1,0:T(8,128)(2,1)S(1)} %copy-done, ...), custom_call_target="tpu_custom_call", output_to_operand_aliasing={{0}: (9, {})} | custom-call | flops 1 | bytes 1 | tf_op jit(solution)/shard_map/last_part/pallas_call | solution.py:108
  (38 shorter events, 0.2 us)
Async XLA Ops:
  7.2 100.6 %all-gather.3.cloned.1.call-start = ((), (), s32[]{:S(2)}) async-start(), calls=%async_computation.6 | async-start | bytes 10485760 | tf_op jit(solution)/shard_map/all_gather | solution.py:475
  13.5 7.5 %collective-permute-start = (f32[32,8,128]{2,1,0:T(8,128)}, f32[32,8,128]{2,1,0:T(8,128)S(1)}, u32[]{:S(2)}, u32[]{:S(2)}) collective-permute-start(f32[32,8,128]{2,1,0:T(8,128)} %get-tuple-element.75), channel_id=1, source_target_pairs={{0,8},{8,0},{1,9},{9,1},{2,10},{10,2},{3,11},{11,3},{4,12},{12,4},... | collective-permute-start | bytes 393224 | tf_op jit(solution)/shard_map/ppermute | solution.py:483
  16.6 17.1 %collective-permute-start.1 = (bf16[512,256]{1,0:T(8,128)(2,1)}, bf16[512,256]{1,0:T(8,128)(2,1)S(1)}, u32[]{:S(2)}, u32[]{:S(2)}) collective-permute-start(bf16[512,256]{1,0:T(8,128)(2,1)} %get-tuple-element.78), channel_id=1, source_target_pairs={{0,2},{2,4},{4,6},{6,0},{1,3},{3,5},{5,7},{7,1},{8,10},{10,12},{12... | collective-permute-start | bytes 786440 | tf_op jit(solution)/shard_map/ppermute | solution.py:482
  18.1 15.6 %collective-permute-start.2 = (bf16[512,256]{1,0:T(8,128)(2,1)}, bf16[512,256]{1,0:T(8,128)(2,1)S(1)}, u32[]{:S(2)}, u32[]{:S(2)}) collective-permute-start(bf16[512,256]{1,0:T(8,128)(2,1)} %get-tuple-element.79), channel_id=1, source_target_pairs={{2,0},{4,2},{6,4},{0,6},{3,1},{5,3},{7,5},{1,7},{10,8},{12,10},{14... | collective-permute-start | bytes 786440 | tf_op jit(solution)/shard_map/ppermute | solution.py:482
  19.0 17.0 %collective-permute-start.3 = (bf16[512,256]{1,0:T(8,128)(2,1)}, bf16[512,256]{1,0:T(8,128)(2,1)S(1)}, u32[]{:S(2)}, u32[]{:S(2)}) collective-permute-start(bf16[512,256]{1,0:T(8,128)(2,1)} %get-tuple-element.80), channel_id=1, source_target_pairs={{0,4},{2,6},{4,0},{6,2},{1,5},{3,7},{5,1},{7,3},{8,12},{10,14},{12... | collective-permute-start | bytes 786440 | tf_op jit(solution)/shard_map/ppermute | solution.py:482
  22.6 17.4 %all-to-all-start = ((f32[32,8,128]{2,1,0:T(8,128)}), f32[32,8,128]{2,1,0:T(8,128)S(1)}, u32[]{:S(2)}, u32[]{:S(2)}) async-start(f32[32,8,128]{2,1,0:T(8,128)} %add.17), calls=%async_computation | async-start | bytes 262144 | tf_op jit(solution)/shard_map/all_to_all | solution.py:458
  33.7 43.8 %copy-start.5 = (bf16[512,256]{1,0:T(8,128)(2,1)}, bf16[512,256]{1,0:T(8,128)(2,1)S(1)}, u32[]{:S(2)}) copy-start(bf16[512,256]{1,0:T(8,128)(2,1)S(1)} %collective-permute-done.1.refs_1_) | copy-start | bytes 786436
  33.7 43.8 %copy-start.6 = (bf16[512,256]{1,0:T(8,128)(2,1)}, bf16[512,256]{1,0:T(8,128)(2,1)S(1)}, u32[]{:S(2)}) copy-start(bf16[512,256]{1,0:T(8,128)(2,1)S(1)} %collective-permute-done.2.refs_2_) | copy-start | bytes 786436
  36.0 41.6 %copy-start.7 = (bf16[512,256]{1,0:T(8,128)(2,1)}, bf16[512,256]{1,0:T(8,128)(2,1)S(1)}, u32[]{:S(2)}) copy-start(bf16[512,256]{1,0:T(8,128)(2,1)S(1)} %collective-permute-done.3.refs_3_) | copy-start | bytes 786436
  69.8 1.8 %copy-start.12 = (f32[32,8,128]{2,1,0:T(8,128)}, f32[32,8,128]{2,1,0:T(8,128)S(1)}, u32[]{:S(2)}) copy-start(f32[32,8,128]{2,1,0:T(8,128)S(1)} %all_to_all.31.own) | copy-start | bytes 393220
  69.8 30.1 %collective-permute-start.6 = (bf16[128,4096]{1,0:T(8,128)(2,1)}, bf16[128,4096]{1,0:T(8,128)(2,1)S(1)}, u32[]{:S(2)}, u32[]{:S(2)}) collective-permute-start(bf16[128,4096]{1,0:T(8,128)(2,1)} %pick_half.1), channel_id=1, source_target_pairs={{0,1},{1,0},{2,3},{3,2},{4,5},{5,4},{6,7},{7,6},{8,9},{9,8},{10,11... | collective-permute-start | bytes 3145736 | tf_op jit(solution)/shard_map/ppermute | solution.py:492
  70.2 1.3 collective-permute-start.4
  71.5 0.7 copy-start.14
  78.3 3.8 %collective-permute-start.5 = (f32[64,8,128]{2,1,0:T(8,128)}, f32[64,8,128]{2,1,0:T(8,128)S(1)}, u32[]{:S(2)}, u32[]{:S(2)}) collective-permute-start(f32[64,8,128]{2,1,0:T(8,128)} %get-tuple-element.91), channel_id=1, source_target_pairs={{0,8},{8,0},{1,9},{9,1},{2,10},{10,2},{3,11},{11,3},{4,12},{12,4},... | collective-permute-start | bytes 786440 | tf_op jit(solution)/shard_map/ppermute | solution.py:497
  83.9 16.0 %all-to-all-start.3 = ((f32[64,8,128]{2,1,0:T(8,128)}), f32[64,8,128]{2,1,0:T(8,128)S(1)}, u32[]{:S(2)}, u32[]{:S(2)}) async-start(f32[64,8,128]{2,1,0:T(8,128)} %add.18), calls=%async_computation.3 | async-start | bytes 524288 | tf_op jit(solution)/shard_map/all_to_all | solution.py:458
  99.9 13.4 %copy-start.8 = (bf16[128,4096]{1,0:T(8,128)(2,1)}, bf16[128,4096]{1,0:T(8,128)(2,1)S(1)}, u32[]{:S(2)}) copy-start(bf16[128,4096]{1,0:T(8,128)(2,1)S(1)} %collective-permute-done.6.w_half) | copy-start | bytes 3145732
  99.9 17.3 %collective-permute-start.7 = (bf16[128,4096]{1,0:T(8,128)(2,1)S(1)}, bf16[128,4096]{1,0:T(8,128)(2,1)S(1)}, u32[]{:S(2)}, u32[]{:S(2)}) collective-permute-start(bf16[128,4096]{1,0:T(8,128)(2,1)S(1)} %collective-permute-done.6.w_half), channel_id=1, source_target_pairs={{0,8},{8,0},{1,9},{9,1},{2,10},{10,2},{3,11},{11,3},{4,12},{12,4},... | collective-permute-start | bytes 3145736 | tf_op jit(solution)/shard_map/ppermute | solution.py:504
  100.9 16.3 %all-to-all-start.4 = ((f32[128,8,128]{2,1,0:T(8,128)}), f32[128,8,128]{2,1,0:T(8,128)S(1)}, u32[]{:S(2)}, u32[]{:S(2)}) async-start(f32[128,8,128]{2,1,0:T(8,128)} %bitcast.13), calls=%async_computation.4 | async-start | bytes 1048576 | tf_op jit(solution)/shard_map/all_to_all | solution.py:458
  113.3 29.6 %collective-permute-start.9 = (bf16[256,1536]{1,0:T(8,128)(2,1)}, bf16[256,1536]{1,0:T(8,128)(2,1)}, u32[]{:S(2)}, u32[]{:S(2)}) collective-permute-start(bf16[256,1536]{1,0:T(8,128)(2,1)} %get-tuple-element.115), channel_id=1, source_target_pairs={{0,1},{1,0},{2,3},{3,2},{4,5},{5,4},{6,7},{7,6},{8,9},{9,8},{10,11... | collective-permute-start | bytes 2359304 | tf_op jit(solution)/shard_map/ppermute | solution.py:510
  117.2 10.0 %copy-start.9 = (bf16[128,4096]{1,0:T(8,128)(2,1)}, bf16[128,4096]{1,0:T(8,128)(2,1)S(1)}, u32[]{:S(2)}) copy-start(bf16[128,4096]{1,0:T(8,128)(2,1)S(1)} %collective-permute-done.7.w_other) | copy-start | bytes 3145732
  118.0 14.3 %all-to-all-start.5 = ((f32[64,8,128]{2,1,0:T(8,128)}), f32[64,8,128]{2,1,0:T(8,128)S(1)}, u32[]{:S(2)}, u32[]{:S(2)}) async-start(f32[64,8,128]{2,1,0:T(8,128)} %bitcast.16), calls=%async_computation.5 | async-start | bytes 524288 | tf_op jit(solution)/shard_map/all_to_all | solution.py:458
  127.2 23.7 %collective-permute-start.10 = (bf16[256,1536]{1,0:T(8,128)(2,1)}, bf16[256,1536]{1,0:T(8,128)(2,1)S(1)}, u32[]{:S(2)}, u32[]{:S(2)}) collective-permute-start(bf16[256,1536]{1,0:T(8,128)(2,1)} %get-tuple-element.120), channel_id=1, source_target_pairs={{0,1},{1,0},{2,3},{3,2},{4,5},{5,4},{6,7},{7,6},{8,9},{9,8},{10,11... | collective-permute-start | bytes 2359304 | tf_op jit(solution)/shard_map/ppermute | solution.py:515
  132.3 10.5 %copy-start.10 = (f32[64,8,128]{2,1,0:T(8,128)}, f32[64,8,128]{2,1,0:T(8,128)S(1)}, u32[]{:S(2)}) copy-start(f32[64,8,128]{2,1,0:T(8,128)S(1)} %all-to-all-done.5.own) | copy-start | bytes 786436
  132.3 10.5 %collective-permute-start.8 = (f32[64,8,128]{2,1,0:T(8,128)S(1)}, f32[64,8,128]{2,1,0:T(8,128)S(1)}, u32[]{:S(2)}, u32[]{:S(2)}) collective-permute-start(f32[64,8,128]{2,1,0:T(8,128)S(1)} %all-to-all-done.5.own), channel_id=1, source_target_pairs={{0,8},{8,0},{1,9},{9,1},{2,10},{10,2},{3,11},{11,3},{4,12},{12,4},... | collective-permute-start | bytes 786440 | tf_op jit(solution)/shard_map/ppermute | solution.py:520
  132.4 29.1 %collective-permute-start.11 = (bf16[256,1024]{1,0:T(8,128)(2,1)}, bf16[256,1024]{1,0:T(8,128)(2,1)S(1)}, u32[]{:S(2)}, u32[]{:S(2)}) collective-permute-start(bf16[256,1024]{1,0:T(8,128)(2,1)} %get-tuple-element.122), channel_id=1, source_target_pairs={{0,1},{1,0},{2,3},{3,2},{4,5},{5,4},{6,7},{7,6},{8,9},{9,8},{10,11... | collective-permute-start | bytes 1572872 | tf_op jit(solution)/shard_map/ppermute | solution.py:519
  142.8 18.7 %copy-start = (bf16[256,1024]{1,0:T(8,128)(2,1)S(1)}, bf16[256,1024]{1,0:T(8,128)(2,1)}, u32[]{:S(2)}) copy-start(bf16[256,1024]{1,0:T(8,128)(2,1)} %get-tuple-element.130.kept) | copy-start | bytes 1572868
  142.8 18.7 %copy-start.2 = (bf16[256,512]{1,0:T(8,128)(2,1)S(1)}, bf16[256,512]{1,0:T(8,128)(2,1)}, u32[]{:S(2)}) copy-start(bf16[256,512]{1,0:T(8,128)(2,1)} %get-tuple-element.132.refs_0_) | copy-start | bytes 786436
  142.8 18.7 %copy-start.4 = (s32[3]{0:T(128)S(1)}, s32[3]{0:T(128)}, u32[]{:S(2)}) copy-start(s32[3]{0:T(128)} %pad_add_fusion.at) | copy-start | bytes 40
  142.8 8.0 %copy-start.13 = (f32[64,8,128]{2,1,0:T(8,128)}, f32[64,8,128]{2,1,0:T(8,128)S(1)}, u32[]{:S(2)}) copy-start(f32[64,8,128]{2,1,0:T(8,128)S(1)} %collective-permute-done.8.other) | copy-start | bytes 786436
  142.9 18.6 %collective-permute-start.12 = (bf16[256,512]{1,0:T(8,128)(2,1)}, bf16[256,512]{1,0:T(8,128)(2,1)S(1)}, u32[]{:S(2)}, u32[]{:S(2)}) collective-permute-start(bf16[256,512]{1,0:T(8,128)(2,1)} %get-tuple-element.124), channel_id=1, source_target_pairs={{2,0},{4,2},{6,4},{0,6},{3,1},{5,3},{7,5},{1,7},{10,8},{12,10},{14... | collective-permute-start | bytes 786440 | tf_op jit(solution)/shard_map/ppermute | solution.py:524
  145.7 15.8 %collective-permute-start.13 = (bf16[256,512]{1,0:T(8,128)(2,1)}, bf16[256,512]{1,0:T(8,128)(2,1)S(1)}, u32[]{:S(2)}, u32[]{:S(2)}) collective-permute-start(bf16[256,512]{1,0:T(8,128)(2,1)} %get-tuple-element.125), channel_id=1, source_target_pairs={{0,2},{2,4},{4,6},{6,0},{1,3},{3,5},{5,7},{7,1},{8,10},{10,12},{12... | collective-permute-start | bytes 786440 | tf_op jit(solution)/shard_map/ppermute | solution.py:524
  145.7 15.8 %collective-permute-start.14 = (bf16[256,512]{1,0:T(8,128)(2,1)}, bf16[256,512]{1,0:T(8,128)(2,1)S(1)}, u32[]{:S(2)}, u32[]{:S(2)}) collective-permute-start(bf16[256,512]{1,0:T(8,128)(2,1)} %get-tuple-element.126), channel_id=1, source_target_pairs={{0,4},{2,6},{4,0},{6,2},{1,5},{3,7},{5,1},{7,3},{8,12},{10,14},{12... | collective-permute-start | bytes 786440 | tf_op jit(solution)/shard_map/ppermute | solution.py:524
  150.9 0.9 copy-start.11
  161.5 1.0 copy-start.1
  162.6 0.9 copy-start.3
Sparse Core Ops, SparseCore 0:
  9.8 94.2 all-gather.2
